TPU v7x, 128 devices: a whole 4x4x4 slice. The times are simulated.
128 devices in a mesh: seq: 16 (over y, z), head: 8 (over x, core).
Axes of the slice: x: 4, y: 4, z: 4, core: 2. Of those that a mesh axis runs over, the one named last changes fastest.
Arguments:
- tokens: bfloat16 [8192, 4096], P('seq'), may hold values from -6 to 6
- w_query: bfloat16 [4096, 4096], P(None, 'head'), may hold values from -0.09375 to 0.09375
- w_key: bfloat16 [4096, 4096], P(None, 'head'), may hold values from -0.09375 to 0.09375
- w_value: bfloat16 [4096, 4096], P(None, 'head'), may hold values from -0.09375 to 0.09375
- w_out: bfloat16 [4096, 4096], P('head'), may hold values from -0.125 to 0.125
- norm_gain: float32 [4096], P('head'), may hold values from 0.1 to 1.9
- level_weights: float32 [21, 32, 8192], P(None, 'head', 'seq'), may hold values from 0.00024414062 to 4, as said below
- prior_states: float32 [4, 32, 128, 128], P(None, 'head'), may hold values from -96 to 96
Outputs:
- layer_out: bfloat16 [8192, 4096], P('seq', 'head')
Inputs may be any that keep to these rules, and one draw needn't show every extreme that they name: `level_weights`: positive.
All inputs are finite; a program needn't handle non-finite values.
Results may differ from a plain program's by a relative error of at most 0.022.
Values may be sent and summed in bfloat16 or wider, within the bound.
A program may use at most 128 MiB of HBM per device.

v0:
```python
import jax
import jax.numpy as jnp
from jax import lax
from jax.sharding import PartitionSpec as P

eps = 1e-06


def unit_heads(tokens, weight, heads, width):
    raw = jnp.dot(tokens, weight, preferred_element_type=jnp.float32)
    raw = raw.reshape(raw.shape[0], heads, width)
    return (raw * lax.rsqrt(jnp.sum(raw * raw, axis=-1, keepdims=True) + eps)).astype(jnp.bfloat16)


def block_attend(query_block, keys, values, lam, pos, cols, shift):
    scores = jnp.einsum("thd,shd->hts", query_block, keys, preferred_element_type=jnp.float32)
    differ = jnp.bitwise_xor(pos[:, None], cols[None, :])
    level = jnp.zeros(differ.shape, jnp.int32)
    for bit in range(shift):
        level = level + (jnp.right_shift(differ, bit) > 0).astype(jnp.int32)
    weight = jnp.zeros(scores.shape, jnp.float32)
    for lv in range(shift + 1):
        weight = weight + jnp.where((level == lv)[None], lam[lv][:, :, None], jnp.float32(0.0))
    causal = cols[None, :] <= pos[:, None]
    mixing = jnp.where(causal[None], weight * scores, jnp.float32(0.0)).astype(jnp.bfloat16)
    return jnp.einsum("hts,shd->thd", mixing, values, preferred_element_type=jnp.float32)


def local_part(query, keys, values, level_weights, shift):
    rows, heads, width = query.shape
    step_rows = min(rows, 512)
    cols = jnp.arange(rows, dtype=jnp.int32)

    def one_block(index):
        start = index * step_rows
        pos = start + jnp.arange(step_rows, dtype=jnp.int32)
        return block_attend(query, keys, values, level_weights, pos, cols, shift)

    outputs = lax.map(one_block, jnp.arange(rows // step_rows, dtype=jnp.int32))
    return outputs.reshape(rows, heads, width)


def per_device(tokens, w_query, w_key, w_value, w_out, norm_gain, level_weights, prior_states):
    rows = tokens.shape[0]
    levels, heads, _ = level_weights.shape
    prior, _, width, _ = prior_states.shape
    shift = rows.bit_length() - 1
    query = unit_heads(tokens, w_query, heads, width)
    keys = unit_heads(tokens, w_key, heads, width)
    values = (
        jnp.dot(tokens, w_value, preferred_element_type=jnp.float32)
        .astype(jnp.bfloat16)
        .reshape(rows, heads, width)
    )
    near = local_part(query, keys, values, level_weights, shift)
    own_state = jnp.einsum("shd,she->hde", keys, values, preferred_element_type=jnp.float32)
    count = lax.axis_size("seq")
    nbits = count.bit_length() - 1
    mine = lax.axis_index("seq")
    level_states = []
    everyone = lax.all_gather(
        own_state[None].astype(jnp.bfloat16), "seq", axis=0, tiled=True
    ).astype(jnp.float32)
    peers = jnp.arange(count, dtype=jnp.int32)
    for bit in range(nbits):
        chosen = (
            (mine >> bit & 1 == 1) & (peers >> bit + 1 == mine >> bit + 1) & (peers >> bit & 1 == 0)
        )
        level_states.append(
            jnp.einsum(
                "n,nhde->hde", chosen.astype(jnp.float32), everyone, precision=lax.Precision.HIGHEST
            )
        )
    picks = [1 + shift + bit for bit in range(nbits)] + [levels - prior + p for p in range(prior)]
    stacked = jnp.stack(level_states + [prior_states[p] for p in range(prior)])
    lam_far = jnp.stack([level_weights[row] for row in picks])
    weighted = lam_far.transpose(0, 2, 1)[..., None] * query.astype(jnp.float32)[None]
    far = jnp.einsum("lthd,lhde->the", weighted, stacked, precision=lax.Precision.HIGHEST)
    mixed = near + far
    scale = lax.rsqrt(jnp.mean(mixed * mixed, axis=-1, keepdims=True) + eps)
    normed = (
        (mixed * scale * norm_gain.reshape(heads, width))
        .astype(jnp.bfloat16)
        .reshape(rows, heads * width)
    )
    partial_out = jnp.dot(normed, w_out, preferred_element_type=jnp.float32)
    return lax.psum_scatter(
        partial_out.astype(jnp.bfloat16), "head", scatter_dimension=1, tiled=True
    )


def solution(mesh):
    placed = (
        P("seq", None),
        P(None, "head"),
        P(None, "head"),
        P(None, "head"),
        P("head", None),
        P("head"),
        P(None, "head", "seq"),
        P(None, "head", None, None),
    )
    return jax.shard_map(
        per_device, mesh=mesh, in_specs=placed, out_specs=P("seq", "head"), check_vma=False
    )
```

profile of v0, /device:TPU:24, one launch (start us, length us, event | category | flops | bytes accessed | tf_op | source)
XLA Modules:
  0.0 141.1 jit_solution(13211411559767700181)
XLA Ops:
  6.5 0.0 all-gather.3.cloned.1.call-start
  6.5 6.0 %convolution_convert_fusion.1 = bf16[512,512]{0,1:T(8,128)(2,1)S(1)} fusion(bf16[512,4096]{1,0:T(8,128)(2,1)} %param.8, bf16[4096,512]{1,0:T(8,128)(2,1)} %param.11), kind=kOutput, calls=%fused_computation.18 | convolution fusion | flops 2147745792 | bytes 8912896 | tf_op jit(solution)/shard_map/dot_general | solution.py:51
  12.5 0.0 copy-done.8
  12.5 0.0 copy-done.9
  12.5 0.0 copy-start.5
  12.5 0.0 copy-start.10
  12.6 2.4 %multiply_reduce_fusion.2 = (f32[512,4]{0,1:T(4,128)S(1)}, f32[512,512]{0,1:T(8,128)S(1)}) fusion(bf16[512,4096]{1,0:T(8,128)(2,1)S(1)} %copy-done.9, bf16[4096,512]{1,0:T(8,128)(2,1)S(1)} %copy-done.8), kind=kOutput, calls=%fused_computation.25 | convolution fusion | flops 2148005888 | bytes 9445376 | tf_op jit(solution)/shard_map/dot_general | solution.py:10
  15.0 0.0 copy-done.10
  15.0 0.0 copy-start.6
  15.0 0.0 copy-start.3
  15.0 3.4 %multiply_reduce_fusion.1 = (f32[512,4]{0,1:T(4,128)S(1)}, f32[512,512]{0,1:T(8,128)}) fusion(bf16[512,4096]{1,0:T(8,128)(2,1)S(1)} %copy-done.9, bf16[4096,512]{1,0:T(8,128)(2,1)S(1)} %copy-done.10), kind=kOutput, calls=%fused_computation.23 | convolution fusion | flops 2148005888 | bytes 9445376 | tf_op jit(solution)/shard_map/dot_general | solution.py:10
  18.4 0.0 copy-done.5
  18.4 2.2 %convolution_convert_fusion.2 = bf16[4,128,128]{2,1,0:T(8,128)(2,1)} fusion(bf16[512,4,128]{0,2,1:T(8,128)(2,1)S(1)} %bitcast.89, f32[512,4,128]{0,2,1:T(8,128)} %bitcast.12, f32[512,4]{0,1:T(4,128)S(1)} %get-tuple-element.54), kind=kOutput, calls=%fused_computation.19 | convolution fusion | flops 67698688 | bytes 1712128 | tf_op jit(solution)/shard_map/shd,she->hde/dot_general | solution.py:56
  20.6 0.0 all-gather.3.cloned.1.call-update
  20.6 0.2 reduce-scatter.2.cloned.1.call-start
  20.8 0.0 copy-done.6
  20.9 0.0 copy-done.3
  20.9 0.3 copy.14
  21.3 0.1 fusion.22
  21.4 1.3 copy.16
  22.7 1.3 broadcast_compare_fusion.9
  24.0 0.6 slice_bitcast_fusion.9
  24.6 1.5 %broadcast_compare_fusion.7 = (pred[512,512]{1,0:T(8,128)(4,1)S(1)}, pred[512,512]{1,0:T(8,128)(4,1)S(1)}) fusion(), kind=kLoop, calls=%fused_computation.45 | loop fusion | flops 9961472 | bytes 524288 | tf_op jit(solution)/shard_map/while/body/eval_jaxpr/eq | solution.py:23
  26.1 1.5 %broadcast_compare_fusion.5 = (pred[512,512]{1,0:T(8,128)(4,1)S(1)}, pred[512,512]{1,0:T(8,128)(4,1)S(1)}) fusion(), kind=kLoop, calls=%fused_computation.43 | loop fusion | flops 9961472 | bytes 524288 | tf_op jit(solution)/shard_map/while/body/eval_jaxpr/eq | solution.py:23
  27.5 2.3 %broadcast_compare_fusion.3 = (pred[512,512]{1,0:T(8,128)(4,1)}, pred[512,512]{1,0:T(8,128)(4,1)}) fusion(), kind=kLoop, calls=%fused_computation.41 | loop fusion | flops 9961472 | bytes 524288 | tf_op jit(solution)/shard_map/while/body/eval_jaxpr/eq | solution.py:23
  29.8 2.3 %broadcast_compare_fusion.1 = (pred[512,512]{1,0:T(8,128)(4,1)}, pred[512,512]{1,0:T(8,128)(4,1)}) fusion(), kind=kLoop, calls=%fused_computation.39 | loop fusion | flops 9961472 | bytes 524288 | tf_op jit(solution)/shard_map/while/body/eval_jaxpr/eq | solution.py:23
  32.1 2.2 %iota_compare_fusion = (pred[512,512]{1,0:T(8,128)(4,1)}, pred[512,512]{1,0:T(8,128)(4,1)}) fusion(), kind=kLoop, calls=%fused_computation.37 | loop fusion | flops 9961472 | bytes 524288 | tf_op jit(solution)/shard_map/while/body/eval_jaxpr/le | solution.py:24
  34.3 9.0 %fusion.4 = f32[4,128,512]{2,1,0:T(8,128)} fusion(bf16[512,4,128]{0,2,1:T(8,128)(2,1)} %bitcast.90, f32[4,512]{1,0:T(4,128)S(1)} %get-tuple-element.20, f32[4,512]{1,0:T(4,128)S(1)} %get-tuple-element.28, f32[4,512]{1,0:T(4,128)S(1)} %get-tuple-element.30, f32[4,512]{1,0:T(4,128)S(1)} %get-tuple-element.32, f32[4,512]{1,0:T(4,128)S(1)} %get-tuple-element.33, ...), kind=kOutput, calls=%fused_computation.6 | convolution fusion | flops 560988160 | bytes 6651904 | tf_op jit(solution)/shard_map/while/body/eval_jaxpr/hts,shd->thd/dot_general | solution.py:26
  43.3 24.3 %all-gather.3.cloned.1.call-done = bf16[64,128,128]{2,1,0:T(8,128)(2,1)} async-done(((bf16[4,128,128]{2,1,0:T(8,128)(2,1)}), bf16[64,128,128]{2,1,0:T(8,128)(2,1)}) %all-gather.3.cloned.1.call-update) | async-done | bytes 2097168 | tf_op jit(solution)/shard_map/all_gather | solution.py:61
  67.6 3.0 %fusion.12 = f32[1,4,128,128]{3,0,2,1:T(1,128)S(1)} fusion(bf16[16,4,128,128]{3,2,1,0:T(8,128)(2,1)} %bitcast.83, pred[]{:T(512)S(6)} %eq.142, s32[]{:T(128)S(6)} %shift_right_arithmetic.533), kind=kOutput, calls=%fused_computation.12 | convolution fusion | flops 2097264 | bytes 2359301 | tf_op jit(solution)/shard_map/n,nhde->hde/dot_general | solution.py:70
  70.6 0.8 copy.22
  71.5 2.9 %fusion.10 = f32[1,4,128,128]{3,0,2,1:T(1,128)S(1)} fusion(bf16[16,4,128,128]{3,2,1,0:T(8,128)(2,1)} %bitcast.84, pred[]{:T(512)S(6)} %eq.146, s32[]{:T(128)S(6)} %shift_right_arithmetic.535), kind=kOutput, calls=%fused_computation.10 | convolution fusion | flops 2097264 | bytes 2359301 | tf_op jit(solution)/shard_map/n,nhde->hde/dot_general | solution.py:70
  74.4 0.8 copy.24
  75.2 1.3 fusion.14
  76.5 0.8 copy.20
  77.4 1.3 fusion.8
  78.6 0.1 copy.26
  78.8 1.1 bitcast_dynamic-update-slice_fusion.3
  79.9 1.0 bitcast_dynamic-update-slice_fusion.2
  80.8 0.0 copy-start.7
  80.9 1.0 bitcast_dynamic-update-slice_fusion.1
  81.9 0.0 copy-start.1
  81.9 0.1 constant_dynamic-update-slice_fusion
  82.0 10.0 %multiply_reduce_fusion = (f32[512,4]{0,1:T(4,128)S(1)}, f32[512,4,128]{0,2,1:T(8,128)S(1)}) fusion(f32[4,128,512]{2,1,0:T(8,128)S(1)} %copy-done.4, f32[8,4,128,128]{2,3,0,1:T(8,128)S(1)} %constant_dynamic-update-slice_fusion, f32[512,4,128]{2,0,1:T(8,128)S(1)} %copy-done.2, f32[8,512,4]{1,0,2:T(8,128)S(1)} %copy.15), kind=kOutput, calls=%fused_computation.21 | convolution fusion | flops 3224107008 | bytes 5316608 | tf_op jit(solution)/shard_map/lthd,lhde->the/dot_general | solution.py:78
  92.0 0.2 multiply_convert_fusion
  92.2 4.3 %convolution_convert_fusion = bf16[512,4096]{1,0:T(8,128)(2,1)} fusion(bf16[512,512]{0,1:T(8,128)(2,1)S(1)} %bitcast.87, bf16[512,4096]{1,0:T(8,128)(2,1)S(1)} %copy-done.1), kind=kOutput, calls=%fused_computation.2 | convolution fusion | flops 2149580800 | bytes 8912896 | tf_op jit(solution)/shard_map/dot_general | solution.py:86
  96.5 0.0 reduce-scatter.2.cloned.1.call-update
  96.5 37.7 %reduce-scatter.2.cloned.1.call-done = bf16[512,512]{1,0:T(8,128)(2,1)} async-done(((bf16[512,4096]{1,0:T(8,128)(2,1)}), bf16[512,512]{1,0:T(8,128)(2,1)}) %reduce-scatter.2.cloned.1.call-update) | async-done | bytes 524304 | tf_op jit(solution)/shard_map/reduce_scatter | solution.py:87
  (16 shorter events, 0.1 us)
Async XLA Ops:
  6.5 61.1 %all-gather.3.cloned.1.call-start = ((), (), s32[]{:S(2)}) async-start(), calls=%async_computation.2 | async-start | bytes 2228224 | tf_op jit(solution)/shard_map/all_gather | solution.py:61
  6.5 6.0 %copy-start.8 = (bf16[4096,512]{1,0:T(8,128)(2,1)S(1)}, bf16[4096,512]{1,0:T(8,128)(2,1)}, u32[]{:S(2)}) copy-start(bf16[4096,512]{1,0:T(8,128)(2,1)} %param.9) | copy-start | bytes 12582916
  6.5 6.0 %copy-start.9 = (bf16[512,4096]{1,0:T(8,128)(2,1)S(1)}, bf16[512,4096]{1,0:T(8,128)(2,1)}, u32[]{:S(2)}) copy-start(bf16[512,4096]{1,0:T(8,128)(2,1)} %param.8) | copy-start | bytes 12582916
  12.5 5.8 %copy-start.5 = (bf16[512,512]{0,1:T(8,128)(2,1)}, bf16[512,512]{0,1:T(8,128)(2,1)S(1)}, u32[]{:S(2)}) copy-start(bf16[512,512]{0,1:T(8,128)(2,1)S(1)} %convolution_convert_fusion.1) | copy-start | bytes 1572868
  12.5 2.4 %copy-start.10 = (bf16[4096,512]{1,0:T(8,128)(2,1)S(1)}, bf16[4096,512]{1,0:T(8,128)(2,1)}, u32[]{:S(2)}) copy-start(bf16[4096,512]{1,0:T(8,128)(2,1)} %param.10) | copy-start | bytes 12582916
  15.0 5.9 %copy-start.6 = (f32[21,4,512]{2,1,0:T(4,128)S(1)}, f32[21,4,512]{2,1,0:T(4,128)}, u32[]{:S(2)}) copy-start(f32[21,4,512]{2,1,0:T(4,128)} %param.14) | copy-start | bytes 516100
  15.0 5.9 %copy-start.3 = (f32[4,4,128,128]{3,2,1,0:T(8,128)S(1)}, f32[4,4,128,128]{3,2,1,0:T(8,128)}, u32[]{:S(2)}) copy-start(f32[4,4,128,128]{3,2,1,0:T(8,128)} %param.15) | copy-start | bytes 3145732
  20.6 113.7 %reduce-scatter.2.cloned.1.call-start = ((), (), s32[]{:S(2)}) async-start(), calls=%async_computation.1 | async-start | bytes 4718592 | tf_op jit(solution)/shard_map/reduce_scatter | solution.py:87
  67.6 7.6 %copy-start = (bf16[64,128,128]{2,1,0:T(8,128)(2,1)S(1)}, bf16[64,128,128]{2,1,0:T(8,128)(2,1)}, u32[]{:S(2)}) copy-start(bf16[64,128,128]{2,1,0:T(8,128)(2,1)} %all-gather.3.cloned.1.call-done) | copy-start | bytes 6291460
  78.6 3.3 %copy-start.2 = (f32[512,4,128]{2,0,1:T(8,128)S(1)}, f32[512,4,128]{2,0,1:T(8,128)}, u32[]{:S(2)}) copy-start(f32[512,4,128]{2,0,1:T(8,128)} %copy.16) | copy-start | bytes 3145732
  78.8 3.2 %copy-start.4 = (f32[4,128,512]{2,1,0:T(8,128)S(1)}, f32[4,128,512]{2,1,0:T(8,128)}, u32[]{:S(2)}) copy-start(f32[4,128,512]{2,1,0:T(8,128)} %fusion.4) | copy-start | bytes 3145732
  80.8 11.1 %copy-start.7 = (f32[512]{0:T(512)S(1)}, f32[512]{0:T(512)}, u32[]{:S(2)}) copy-start(f32[512]{0:T(512)} %param.13) | copy-start | bytes 6148
  81.9 10.3 %copy-start.1 = (bf16[512,4096]{1,0:T(8,128)(2,1)S(1)}, bf16[512,4096]{1,0:T(8,128)(2,1)}, u32[]{:S(2)}) copy-start(bf16[512,4096]{1,0:T(8,128)(2,1)} %param.12) | copy-start | bytes 12582916
Sparse Core Ops, SparseCore 0:
  20.7 46.8 all-gather.2
  96.7 37.5 reduce-scatter.1
where the time goes:
time: 142 us; the launch traced here: 141 us
  waiting for transfers between devices  62.1 us (44%)
  matrix products  45.8 us (32%)
  between operations  13.7 us (10%)
  other arithmetic  11.3 us (8%)
  local copies, waits for them, and re-layouts  8.09 us (6%)
    reduce_scatter x1, waiting for transfers between devices, per_device(): lax.psum_scatter(partial_out.astype(jnp.bfloat16), 'head', scatter_dimens...  37.7 us
    all_gather x1, waiting for transfers between devices, per_device(): lax.all_gather(own_state[None].astype(jnp.bfloat16), 'seq', axis=0, tiled...  24.3 us
    dot_general x1, matrix products, per_device(): jnp.einsum('lthd,lhde->the', weighted, stacked, precision=lax.Precision.H...  9.99 us
    dot_general x1, matrix products, block_attend(): jnp.einsum('hts,shd->thd', mixing, values, preferred_element_type=jnp.flo...  9 us
    eq x5, other arithmetic, block_attend(): level == lv  8.75 us
    dot_general x4, matrix products, per_device(): jnp.einsum('n,nhde->hde', chosen.astype(jnp.float32), everyone, precision...  8.51 us
    dot_general x1, matrix products, per_device(): jnp.dot(tokens, w_value, preferred_element_type=jnp.float32)  5.97 us
    dot_general x2, matrix products, unit_heads(): raw = jnp.dot(tokens, weight, preferred_element_type=jnp.float32)  5.75 us
  transfers between devices with their start and end apart: 2, of which 2 were waited for; matrix products, arithmetic and copies ran while one was open for 16% of the time, Pallas kernels for 0%

commit v1 on v0

v1 whole, which is shorter than its diff:
```python
import functools

import jax
import jax.numpy as jnp
from jax import lax
from jax.experimental import pallas as pl
from jax.experimental.pallas import tpu as pltpu
from jax.sharding import PartitionSpec as P

MESH = pl.DeviceIdType.MESH
F32 = jnp.float32
BF16 = jnp.bfloat16
eps = 1e-06

ROWS, D, HEADS, DH = 512, 4096, 4, 128
LEVELS, PRIOR = 21, 4
KC = 1024
NK = D // KC
CH = 128
NC = ROWS // CH
NBITS = 4
SHIFT = 9


def dot(a, b):
    return jnp.dot(a, b, preferred_element_type=F32)


def kernel(
    tok_hbm, wq_hbm, wk_hbm, wv_hbm, wo_hbm, gain_hbm, lam_hbm, prior_hbm, out_hbm,
    tok, wq, wk, wv, wo, gain, lam_raw, lam, prior,
    acc_a, acc_b, k_s, vt_s, qt_s, chunk_st, state, y_s, normed,
    st_send, st_recv, sib_send, sib_recv, own_c, d2_send, d2_recv, al_send, al_recv, co_send, co_recv, out_v,
    tok_sem, w_sem, wo_sem, misc_sem, out_sem, st_ss, st_rs, sib_ss, sib_rs, x_ss, x_rs,
):
    s_id = lax.axis_index("seq")
    h_id = lax.axis_index("head")
    x_id, c_id = h_id // 2, h_id % 2
    y_id, z_id = s_id // 4, s_id % 4
    sib = (s_id, x_id * 2 + (1 - c_id))
    right = (s_id, ((x_id + 1) % 4) * 2 + c_id)
    left = (s_id, ((x_id + 3) % 4) * 2 + c_id)
    partners = [
        (y_id * 4 + (z_id + 1 - 2 * (z_id % 2)), h_id),
        (y_id * 4 + (3 - z_id), h_id),
        ((y_id + 1 - 2 * (y_id % 2)) * 4 + z_id, h_id),
        ((3 - y_id) * 4 + z_id, h_id),
    ]
    bits = [z_id % 2, z_id // 2, y_id % 2, y_id // 2]

    barrier = pltpu.get_barrier_semaphore()
    for dev in partners + [sib, right, left]:
        pl.semaphore_signal(barrier, inc=1, device_id=dev, device_id_type=MESH)

    tok_cp = [
        pltpu.make_async_copy(tok_hbm.at[:, pl.ds(k * KC, KC)], tok.at[k], tok_sem.at[k])
        for k in range(NK)
    ]

    def w_cp(i, src, dst, p, k):
        return pltpu.make_async_copy(
            src.at[pl.ds(k * KC, KC), pl.ds(p * 256, 256)],
            dst.at[p, pl.ds(k * KC, KC), :],
            w_sem.at[i, p, k],
        )

    for k in range(NK):
        tok_cp[k].start()
        w_cp(0, wk_hbm, wk, 0, k).start()
        w_cp(1, wv_hbm, wv, 0, k).start()
    for k in range(NK):
        w_cp(0, wk_hbm, wk, 1, k).start()
        w_cp(1, wv_hbm, wv, 1, k).start()
    for p in range(2):
        for k in range(NK):
            w_cp(2, wq_hbm, wq, p, k).start()
    lam_cp = pltpu.make_async_copy(lam_hbm, lam_raw, misc_sem.at[0])
    prior_cp = pltpu.make_async_copy(prior_hbm, prior, misc_sem.at[1])
    gain_cp = pltpu.make_async_copy(gain_hbm, gain, misc_sem.at[2])
    lam_cp.start()
    prior_cp.start()
    gain_cp.start()
    wo_cp = [
        pltpu.make_async_copy(wo_hbm.at[:, pl.ds(b * 512, 512)], wo.at[b], wo_sem.at[b])
        for b in range(8)
    ]
    for b in range(8):
        wo_cp[b].start()

    def st_copy(j, h):
        return pltpu.make_async_remote_copy(
            src_ref=st_send.at[j, h], dst_ref=st_recv.at[j, h],
            send_sem=st_ss.at[j, h], recv_sem=st_rs.at[j, h],
            device_id=partners[j], device_id_type=MESH,
        )

    def project(p, first, weights, accs, with_tok):
        for acc in accs:
            acc[...] = jnp.zeros_like(acc)

        def step(k, _):
            if with_tok:
                pltpu.make_async_copy(tok_hbm.at[:, pl.ds(0, KC)], tok.at[k], tok_sem.at[k]).wait()
            for n, (src, w, acc) in enumerate(zip((wk_hbm, wv_hbm, wq_hbm)[first:], weights, accs)):
                w_cp(first + n, src, w, p, k).wait()
                rows = pl.ds(pl.multiple_of(k * KC, KC), KC)
                for m in range(2):
                    acc[pl.ds(m * 256, 256), :] += dot(tok[k, pl.ds(m * 256, 256), :], w[p, rows, :])
            return 0

        lax.fori_loop(0, NK, step, 0)

    def kv_post(p):
        for i in range(2):
            h = 2 * p + i
            raw = acc_a[:, i * DH:(i + 1) * DH]
            k_s[h] = (raw * lax.rsqrt(jnp.sum(raw * raw, axis=-1, keepdims=True) + eps)).astype(BF16)
            vt_s[h] = acc_b[:, i * DH:(i + 1) * DH].T.astype(BF16)
            st = [
                dot(vt_s[h, :, c * CH:(c + 1) * CH], k_s[h, c * CH:(c + 1) * CH, :])
                for c in range(NC)
            ]
            s01 = st[0] + st[1]
            chunk_st[h, 0] = st[0].astype(BF16)
            chunk_st[h, 1] = s01.astype(BF16)
            chunk_st[h, 2] = st[2].astype(BF16)
            total = s01 + (st[2] + st[3])
            state[h] = total
            st_send[0, h] = total.astype(BF16)
            st_copy(0, h).start()

    def advance(j, h):
        st_copy(j, h).wait_recv()
        total = state[h] + st_recv[j, h].astype(F32)
        state[h] = total
        st_send[j + 1, h] = total.astype(BF16)
        st_copy(j + 1, h).start()

    def q_post(p):
        for i in range(2):
            h = 2 * p + i
            raw = acc_a[:, i * DH:(i + 1) * DH].T
            qt_s[h] = (raw * lax.rsqrt(jnp.sum(raw * raw, axis=0, keepdims=True) + eps)).astype(BF16)

    srow = lax.broadcasted_iota(jnp.int32, (CH, CH), 0)
    tcol = lax.broadcasted_iota(jnp.int32, (CH, CH), 1)

    def near(h):
        differ = srow ^ tcol
        level = jnp.zeros((CH, CH), jnp.int32)
        for bit in range(7):
            level = level + (differ >= (1 << bit)).astype(jnp.int32)
        level = jnp.where(srow <= tcol, level, 99)
        q_full = qt_s[h]
        qf = q_full.astype(F32)
        b_all = jnp.concatenate(
            [(lam[h, LEVELS - PRIOR + p:LEVELS - PRIOR + p + 1, :] * qf).astype(BF16) for p in range(PRIOR)], axis=0
        )
        a_all = jnp.concatenate([prior[p, h].T.astype(BF16) for p in range(PRIOR)], axis=1)
        y_s[h] = dot(a_all, b_all)
        l8 = (lam[h, 8:9, :] * qf).astype(BF16)
        l9 = (lam[h, 9:10, :] * qf).astype(BF16)
        for c in range(NC):
            cols = slice(c * CH, (c + 1) * CH)
            scores = dot(k_s[h, cols, :], q_full[:, cols])
            weight = jnp.zeros((CH, CH), F32)
            for lv in range(8):
                weight = jnp.where(level == lv, lam[h, lv:lv + 1, cols], weight)
            mix = (weight * scores).astype(BF16)
            y = dot(vt_s[h, :, cols], mix)
            if c % 2 == 1:
                y = y + dot(chunk_st[h, 0 if c == 1 else 2], l8[:, cols])
            if c >= 2:
                y = y + dot(chunk_st[h, 1], l9[:, cols])
            y_s[h, :, cols] += y

    def carry(j, h):
        flag = bits[j].astype(F32)
        row = lam[h, 1 + SHIFT + j:2 + SHIFT + j, :] * flag
        return dot(st_recv[j, h], (row * qt_s[h].astype(F32)).astype(BF16))

    def finish(h):
        st_copy(3, h).wait_recv()
        y = y_s[h] + carry(0, h) + carry(1, h) + carry(2, h) + carry(3, h)
        scale = lax.rsqrt(jnp.sum(y * y, axis=0, keepdims=True) * (1.0 / DH) + eps)
        cols = slice(h * DH, (h + 1) * DH)
        normed[:, cols] = ((y * scale).T * gain[0:1, cols]).astype(BF16)

    project(0, 0, (wk, wv), (acc_a, acc_b), True)
    pl.semaphore_wait(barrier, 7)
    kv_post(0)
    project(1, 0, (wk, wv), (acc_a, acc_b), False)
    for h in (0, 1):
        advance(0, h)
    kv_post(1)
    lam_cp.wait()
    for h in range(HEADS):
        lam[h] = lam_raw[:, h, :]
    project(0, 2, (wq,), (acc_a,), False)
    q_post(0)
    for h in (0, 1):
        advance(1, h)
    for h in (2, 3):
        advance(0, h)
    project(1, 2, (wq,), (acc_a,), False)
    q_post(1)
    prior_cp.wait()
    for h in (0, 1):
        advance(2, h)
    for h in (2, 3):
        advance(1, h)
    near(0)
    near(1)
    for h in (2, 3):
        advance(2, h)
    near(2)
    near(3)
    gain_cp.wait()
    for h in range(HEADS):
        finish(h)
    for b in range(8):
        wo_cp[b].wait()

    HALF = 256

    def rows_of(half):
        return pl.ds(half * HALF, HALF)

    def sib_copy(o, half):
        return pltpu.make_async_remote_copy(
            src_ref=sib_send.at[o, half], dst_ref=sib_recv.at[o, half],
            send_sem=sib_ss.at[o, half], recv_sem=sib_rs.at[o, half],
            device_id=sib, device_id_type=MESH,
        )

    def block(o, c):
        return ((x_id + o) % 4) * 2 + c

    def for_sib(o):
        w = wo.at[block(o, 1 - c_id)]
        for half in range(2):
            sib_send[o, half] = dot(normed[rows_of(half), :], w[...]).astype(BF16)
            sib_copy(o, half).start()

    def chip_sum(o, half):
        part = dot(normed[rows_of(half), :], wo[block(o, c_id)])
        sib_copy(o, half).wait_recv()
        return part + sib_recv[o, half].astype(F32)

    bufs = ((d2_send, d2_recv), (al_send, al_recv), (co_send, co_recv))

    def x_copy(kind, way, n):
        src, dst = bufs[kind]
        return pltpu.make_async_remote_copy(
            src_ref=src.at[way, n], dst_ref=dst.at[way, n],
            send_sem=x_ss.at[kind, way, n], recv_sem=x_rs.at[kind, way, n],
            device_id=right if way == 0 else left, device_id_type=MESH,
        )

    NS = d2_send.shape[1]
    SUB = HALF // NS

    for_sib(2)
    for_sib(1)
    for_sib(3)
    for way in range(2):
        tot = chip_sum(2, way).astype(BF16)
        for n in range(NS):
            d2_send[way, n] = tot[n * SUB:(n + 1) * SUB]
            x_copy(0, way, n).start()
    for_sib(0)
    for way in range(2):
        o = 1 if way == 0 else 3
        tot = chip_sum(o, 1 - way).astype(BF16)
        for n in range(NS):
            al_send[way, n] = tot[n * SUB:(n + 1) * SUB]
            x_copy(1, way, n).start()
        own_c[1 + way] = chip_sum(o, way)
    for half in range(2):
        own_c[0 if half == 0 else 3] = chip_sum(0, half)
    for n in range(NS):
        for way in range(2):
            x_copy(0, way, n).wait_recv()
            co_send[way, n] = (
                own_c[1 + way, n * SUB:(n + 1) * SUB, :] + d2_recv[way, n].astype(F32)
            ).astype(BF16)
            x_copy(2, way, n).start()
    out_cps = []
    for n in range(NS):
        for half in range(2):
            x_copy(1, 1 - half, n).wait_recv()
            x_copy(2, half, n).wait_recv()
            mine = own_c[0 if half == 0 else 3, n * SUB:(n + 1) * SUB, :]
            out_v[half, n] = (mine + al_recv[1 - half, n].astype(F32) + co_recv[half, n].astype(F32)).astype(BF16)
            cp = pltpu.make_async_copy(
                out_v.at[half, n], out_hbm.at[pl.ds(half * HALF + n * SUB, SUB), :], out_sem.at[half, n]
            )
            cp.start()
            out_cps.append(cp)
    for cp in out_cps:
        cp.wait()
    for j in range(NBITS):
        for h in range(HEADS):
            st_copy(j, h).wait_send()
    for o in range(4):
        for half in range(2):
            sib_copy(o, half).wait_send()
    for kind in range(3):
        for way in range(2):
            for n in range(NS):
                x_copy(kind, way, n).wait_send()


def per_device(tokens, w_query, w_key, w_value, w_out, norm_gain, level_weights, prior_states):
    NS = 2
    SUB = 256 // NS
    half = (2, NS, SUB, 512)
    scratch = [
        pltpu.VMEM((NK, ROWS, KC), BF16),
        pltpu.VMEM((2, D, 256), BF16),
        pltpu.VMEM((2, D, 256), BF16),
        pltpu.VMEM((2, D, 256), BF16),
        pltpu.VMEM((8, 512, 512), BF16),
        pltpu.VMEM((1, 512), F32),
        pltpu.VMEM((LEVELS, HEADS, ROWS), F32),
        pltpu.VMEM((HEADS, LEVELS, ROWS), F32),
        pltpu.VMEM((PRIOR, HEADS, DH, DH), F32),
        pltpu.VMEM((ROWS, 256), F32),
        pltpu.VMEM((ROWS, 256), F32),
        pltpu.VMEM((HEADS, ROWS, DH), BF16),
        pltpu.VMEM((HEADS, DH, ROWS), BF16),
        pltpu.VMEM((HEADS, DH, ROWS), BF16),
        pltpu.VMEM((HEADS, 3, DH, DH), BF16),
        pltpu.VMEM((HEADS, DH, DH), F32),
        pltpu.VMEM((HEADS, DH, ROWS), F32),
        pltpu.VMEM((ROWS, 512), BF16),
        pltpu.VMEM((NBITS, HEADS, DH, DH), BF16),
        pltpu.VMEM((NBITS, HEADS, DH, DH), BF16),
        pltpu.VMEM((4, 2, 256, 512), BF16),
        pltpu.VMEM((4, 2, 256, 512), BF16),
        pltpu.VMEM((4, 256, 512), F32),
        pltpu.VMEM(half, BF16),
        pltpu.VMEM(half, BF16),
        pltpu.VMEM(half, BF16),
        pltpu.VMEM(half, BF16),
        pltpu.VMEM(half, BF16),
        pltpu.VMEM(half, BF16),
        pltpu.VMEM(half, BF16),
        pltpu.SemaphoreType.DMA((NK,)),
        pltpu.SemaphoreType.DMA((3, 2, NK)),
        pltpu.SemaphoreType.DMA((8,)),
        pltpu.SemaphoreType.DMA((3,)),
        pltpu.SemaphoreType.DMA((2, NS)),
        pltpu.SemaphoreType.DMA((NBITS, HEADS)),
        pltpu.SemaphoreType.DMA((NBITS, HEADS)),
        pltpu.SemaphoreType.DMA((4, 2)),
        pltpu.SemaphoreType.DMA((4, 2)),
        pltpu.SemaphoreType.DMA((3, 2, NS)),
        pltpu.SemaphoreType.DMA((3, 2, NS)),
    ]
    return pl.pallas_call(
        kernel,
        out_shape=jax.ShapeDtypeStruct((ROWS, 512), BF16),
        in_specs=[pl.BlockSpec(memory_space=pl.ANY)] * 8,
        out_specs=pl.BlockSpec(memory_space=pl.ANY),
        scratch_shapes=scratch,
        compiler_params=pltpu.CompilerParams(
            collective_id=0, has_side_effects=True, vmem_limit_bytes=58 << 20
        ),
        cost_estimate=pl.CostEstimate(flops=9_500_000_000, bytes_accessed=22_000_000, transcendentals=0),
    )(tokens, w_query, w_key, w_value, w_out, norm_gain.reshape(1, 512), level_weights, prior_states)


def solution(mesh):
    placed = (
        P("seq", None),
        P(None, "head"),
        P(None, "head"),
        P(None, "head"),
        P("head", None),
        P("head"),
        P(None, "head", "seq"),
        P(None, "head", None, None),
    )
    return jax.shard_map(
        per_device, mesh=mesh, in_specs=placed, out_specs=P("seq", "head"), check_vma=False
    )
```

time: 142 us -> 57.6 us (0.41)
  the two profiles are of different devices: /device:TPU:24 before, /device:TPU:1 now
where the time goes in v1:
time: 57.6 us; the launch traced here: 57.4 us
  Pallas kernels  55.6 us (97%)
  local copies, waits for them, and re-layouts  1.87 us (3%)
    pallas_call x1, Pallas kernels, per_device(): pl.pallas_call(kernel, out_shape=jax.ShapeDtypeStruct((ROWS, 512), BF16),...  55.6 us
    unnamed x1, local copies, waits for them, and re-layouts  1.87 us

profile of v1, /device:TPU:1, one launch (start us, length us, event | category | flops | bytes accessed | tf_op | source)
XLA Modules:
  0.0 57.4 jit_solution(7830182987970843371)
XLA Ops:
  0.0 55.6 %shard_map.82 = bf16[512,512]{1,0:T(8,128)(2,1)} custom-call(bf16[512,4096]{1,0:T(8,128)(2,1)} %tok_hbm.1, bf16[4096,512]{1,0:T(8,128)(2,1)} %wq_hbm.1, bf16[4096,512]{1,0:T(8,128)(2,1)} %wk_hbm.1, bf16[4096,512]{1,0:T(8,128)(2,1)} %wv_hbm.1, bf16[512,4096]{1,0:T(8,128)(2,1)} %wo_hbm.1, f32[1,512]{1,0:T(1,128)} %bitcast.1, f32[21,4,512]{2,1,0:T(4,128)} %lam_hbm.1, ...), custom_call_target="tpu_custom_call" | custom-call | flops 9500000256 | bytes 22000000 | tf_op jit(solution)/shard_map/pallas_call | solution.py:361
  55.6 1.9 %copy.10 = bf16[512,512]{1,0:T(8,128)(2,1)} copy(bf16[512,512]{1,0:T(8,128)(2,1)} %shard_map.82) | data formatting | bytes 1048576

commit v2 on v1

--- a/solution.py
+++ b/solution.py
@@ -14,11 +14,9 @@
 
 ROWS, D, HEADS, DH = 512, 4096, 4, 128
 LEVELS, PRIOR = 21, 4
-KC = 1024
-NK = D // KC
 CH = 128
 NC = ROWS // CH
-NBITS = 4
+FIRST = ((0, 1024), (1024, 1024), (2048, 2048))
 SHIFT = 9
 
 
@@ -30,8 +28,8 @@
     tok_hbm, wq_hbm, wk_hbm, wv_hbm, wo_hbm, gain_hbm, lam_hbm, prior_hbm, out_hbm,
     tok, wq, wk, wv, wo, gain, lam_raw, lam, prior,
     acc_a, acc_b, k_s, vt_s, qt_s, chunk_st, state, y_s, normed,
-    st_send, st_recv, sib_send, sib_recv, own_c, d2_send, d2_recv, al_send, al_recv, co_send, co_recv, out_v,
-    tok_sem, w_sem, wo_sem, misc_sem, out_sem, st_ss, st_rs, sib_ss, sib_rs, x_ss, x_rs,
+    z_send, z_recv, y_send, y_recv, sib_send, sib_recv, own_c, d2_send, d2_recv, al_send, al_recv, co_send, co_recv, out_v,
+    tok_sem, w_sem, wo_sem, misc_sem, out_sem, z_ss, z_rs, y_ss, y_rs, sib_ss, sib_rs, x_ss, x_rs,
 ):
     s_id = lax.axis_index("seq")
     h_id = lax.axis_index("head")
@@ -40,75 +38,60 @@
     sib = (s_id, x_id * 2 + (1 - c_id))
     right = (s_id, ((x_id + 1) % 4) * 2 + c_id)
     left = (s_id, ((x_id + 3) % 4) * 2 + c_id)
-    partners = [
-        (y_id * 4 + (z_id + 1 - 2 * (z_id % 2)), h_id),
-        (y_id * 4 + (3 - z_id), h_id),
-        ((y_id + 1 - 2 * (y_id % 2)) * 4 + z_id, h_id),
-        ((3 - y_id) * 4 + z_id, h_id),
-    ]
-    bits = [z_id % 2, z_id // 2, y_id % 2, y_id // 2]
 
     barrier = pltpu.get_barrier_semaphore()
-    for dev in partners + [sib, right, left]:
+    for dev in [sib, right, left]:
         pl.semaphore_signal(barrier, inc=1, device_id=dev, device_id_type=MESH)
-
-    tok_cp = [
-        pltpu.make_async_copy(tok_hbm.at[:, pl.ds(k * KC, KC)], tok.at[k], tok_sem.at[k])
-        for k in range(NK)
-    ]
-
-    def w_cp(i, src, dst, p, k):
+    for d in range(1, 4):
+        pl.semaphore_signal(barrier, inc=1, device_id=(y_id * 4 + (z_id + d) % 4, h_id), device_id_type=MESH)
+        pl.semaphore_signal(barrier, inc=1, device_id=(((y_id + d) % 4) * 4 + z_id, h_id), device_id_type=MESH)
+
+    def tok_cp(i):
+        cols = pl.ds(*FIRST[i])
+        return pltpu.make_async_copy(tok_hbm.at[:, cols], tok.at[:, cols], tok_sem.at[i])
+
+    def w_cp(n, p, i):
+        src, dst = ((wk_hbm, wk), (wv_hbm, wv), (wq_hbm, wq))[n]
+        rows = pl.ds(*FIRST[i])
         return pltpu.make_async_copy(
-            src.at[pl.ds(k * KC, KC), pl.ds(p * 256, 256)],
-            dst.at[p, pl.ds(k * KC, KC), :],
-            w_sem.at[i, p, k],
-        )
-
-    for k in range(NK):
-        tok_cp[k].start()
-        w_cp(0, wk_hbm, wk, 0, k).start()
-        w_cp(1, wv_hbm, wv, 0, k).start()
-    for k in range(NK):
-        w_cp(0, wk_hbm, wk, 1, k).start()
-        w_cp(1, wv_hbm, wv, 1, k).start()
-    for p in range(2):
-        for k in range(NK):
-            w_cp(2, wq_hbm, wq, p, k).start()
+            src.at[rows, pl.ds(p * 256, 256)], dst.at[p, rows, :], w_sem.at[n, p, i]
+        )
+
+    NF = len(FIRST)
+
+    def start_w(n, p):
+        for i in range(NF):
+            w_cp(n, p, i).start()
+
+    def wait_w(n, p):
+        for i in range(NF):
+            w_cp(n, p, i).wait()
+
     lam_cp = pltpu.make_async_copy(lam_hbm, lam_raw, misc_sem.at[0])
     prior_cp = pltpu.make_async_copy(prior_hbm, prior, misc_sem.at[1])
     gain_cp = pltpu.make_async_copy(gain_hbm, gain, misc_sem.at[2])
-    lam_cp.start()
-    prior_cp.start()
-    gain_cp.start()
     wo_cp = [
         pltpu.make_async_copy(wo_hbm.at[:, pl.ds(b * 512, 512)], wo.at[b], wo_sem.at[b])
         for b in range(8)
     ]
-    for b in range(8):
-        wo_cp[b].start()
-
-    def st_copy(j, h):
+
+    def z_copy(d, h):
         return pltpu.make_async_remote_copy(
-            src_ref=st_send.at[j, h], dst_ref=st_recv.at[j, h],
-            send_sem=st_ss.at[j, h], recv_sem=st_rs.at[j, h],
-            device_id=partners[j], device_id_type=MESH,
-        )
-
-    def project(p, first, weights, accs, with_tok):
-        for acc in accs:
-            acc[...] = jnp.zeros_like(acc)
-
-        def step(k, _):
-            if with_tok:
-                pltpu.make_async_copy(tok_hbm.at[:, pl.ds(0, KC)], tok.at[k], tok_sem.at[k]).wait()
-            for n, (src, w, acc) in enumerate(zip((wk_hbm, wv_hbm, wq_hbm)[first:], weights, accs)):
-                w_cp(first + n, src, w, p, k).wait()
-                rows = pl.ds(pl.multiple_of(k * KC, KC), KC)
-                for m in range(2):
-                    acc[pl.ds(m * 256, 256), :] += dot(tok[k, pl.ds(m * 256, 256), :], w[p, rows, :])
-            return 0
-
-        lax.fori_loop(0, NK, step, 0)
+            src_ref=z_send.at[h], dst_ref=z_recv.at[d, h], send_sem=z_ss.at[d, h], recv_sem=z_rs.at[d, h],
+            device_id=(y_id * 4 + (z_id + 1 + d) % 4, h_id), device_id_type=MESH,
+        )
+
+    def y_copy(d, h):
+        return pltpu.make_async_remote_copy(
+            src_ref=y_send.at[h], dst_ref=y_recv.at[d, h], send_sem=y_ss.at[d, h], recv_sem=y_rs.at[d, h],
+            device_id=(((y_id + 1 + d) % 4) * 4 + z_id, h_id), device_id_type=MESH,
+        )
+
+    def z_sends(d):
+        return (y_id < 3) | (z_id + 1 + d < 4)
+
+    def z_comes(d):
+        return (y_id < 3) | (z_id > d)
 
     def kv_post(p):
         for i in range(2):
@@ -126,15 +109,27 @@
             chunk_st[h, 2] = st[2].astype(BF16)
             total = s01 + (st[2] + st[3])
             state[h] = total
-            st_send[0, h] = total.astype(BF16)
-            st_copy(0, h).start()
-
-    def advance(j, h):
-        st_copy(j, h).wait_recv()
-        total = state[h] + st_recv[j, h].astype(F32)
-        state[h] = total
-        st_send[j + 1, h] = total.astype(BF16)
-        st_copy(j + 1, h).start()
+            z_send[h] = total.astype(BF16)
+            for d in range(3):
+                @pl.when(z_sends(d))
+                def _():
+                    z_copy(d, h).start()
+
+    def pass_on(h):
+        for d in range(3):
+            @pl.when(z_comes(d))
+            def _():
+                z_copy(d, h).wait_recv()
+
+        @pl.when(y_id < 3)
+        def _():
+            y_send[h] = (
+                state[h] + (z_recv[0, h].astype(F32) + z_recv[1, h].astype(F32) + z_recv[2, h].astype(F32))
+            ).astype(BF16)
+            for d in range(3):
+                @pl.when(y_id + 1 + d < 4)
+                def _():
+                    y_copy(d, h).start()
 
     def q_post(p):
         for i in range(2):
@@ -174,47 +169,83 @@
                 y = y + dot(chunk_st[h, 1], l9[:, cols])
             y_s[h, :, cols] += y
 
-    def carry(j, h):
-        flag = bits[j].astype(F32)
-        row = lam[h, 1 + SHIFT + j:2 + SHIFT + j, :] * flag
-        return dot(st_recv[j, h], (row * qt_s[h].astype(F32)).astype(BF16))
+    def far(recv, at, level, h):
+        qf = qt_s[h].astype(F32)
+        low, high = lam[h, level:level + 1, :], lam[h, level + 1:level + 2, :]
+        for d in range(3):
+            @pl.when(at > d)
+            def _():
+                if d == 0:
+                    odd = (at % 2).astype(F32)
+                    row = odd * low + (1.0 - odd) * high
+                else:
+                    row = high
+                y_s[h] += dot(recv[d, h], (row * qf).astype(BF16))
 
     def finish(h):
-        st_copy(3, h).wait_recv()
-        y = y_s[h] + carry(0, h) + carry(1, h) + carry(2, h) + carry(3, h)
+        for d in range(3):
+            @pl.when(y_id > d)
+            def _():
+                y_copy(d, h).wait_recv()
+        far(y_recv, y_id, SHIFT + 3, h)
+        y = y_s[h]
         scale = lax.rsqrt(jnp.sum(y * y, axis=0, keepdims=True) * (1.0 / DH) + eps)
         cols = slice(h * DH, (h + 1) * DH)
         normed[:, cols] = ((y * scale).T * gain[0:1, cols]).astype(BF16)
 
-    project(0, 0, (wk, wv), (acc_a, acc_b), True)
-    pl.semaphore_wait(barrier, 7)
+    tok_cp(0).start()
+    w_cp(0, 0, 0).start()
+    w_cp(1, 0, 0).start()
+    for i in range(1, NF):
+        tok_cp(i).start()
+        w_cp(0, 0, i).start()
+        w_cp(1, 0, i).start()
+    for i in range(NF):
+        rows = pl.ds(*FIRST[i])
+        tok_cp(i).wait()
+        for n, (w, acc) in enumerate(((wk, acc_a), (wv, acc_b))):
+            w_cp(n, 0, i).wait()
+            part = dot(tok[:, rows], w[0, rows, :])
+            if i == 0:
+                acc[...] = part
+            else:
+                acc[...] += part
+        if i == 0:
+            start_w(0, 1)
+            start_w(1, 1)
+        if i == 1:
+            start_w(2, 0)
+            start_w(2, 1)
+    lam_cp.start()
+    prior_cp.start()
+    gain_cp.start()
+    pl.semaphore_wait(barrier, 9)
     kv_post(0)
-    project(1, 0, (wk, wv), (acc_a, acc_b), False)
-    for h in (0, 1):
-        advance(0, h)
+    for n, (w, acc) in enumerate(((wk, acc_a), (wv, acc_b))):
+        wait_w(n, 1)
+        acc[...] = dot(tok[...], w[1])
+    for b in range(8):
+        wo_cp[b].start()
     kv_post(1)
     lam_cp.wait()
     for h in range(HEADS):
         lam[h] = lam_raw[:, h, :]
-    project(0, 2, (wq,), (acc_a,), False)
-    q_post(0)
-    for h in (0, 1):
-        advance(1, h)
-    for h in (2, 3):
-        advance(0, h)
-    project(1, 2, (wq,), (acc_a,), False)
-    q_post(1)
+    for p in range(2):
+        wait_w(2, p)
+        acc_a[...] = dot(tok[...], wq[p])
+        q_post(p)
+        if p == 0:
+            for h in (0, 1):
+                pass_on(h)
     prior_cp.wait()
-    for h in (0, 1):
-        advance(2, h)
-    for h in (2, 3):
-        advance(1, h)
     near(0)
     near(1)
     for h in (2, 3):
-        advance(2, h)
+        pass_on(h)
     near(2)
     near(3)
+    for h in range(HEADS):
+        far(z_recv, z_id, SHIFT + 1, h)
     gain_cp.wait()
     for h in range(HEADS):
         finish(h)
@@ -274,11 +305,13 @@
         tot = chip_sum(o, 1 - way).astype(BF16)
         for n in range(NS):
             al_send[way, n] = tot[n * SUB:(n + 1) * SUB]
-            x_copy(1, way, n).start()
         own_c[1 + way] = chip_sum(o, way)
     for half in range(2):
         own_c[0 if half == 0 else 3] = chip_sum(0, half)
     for n in range(NS):
+        for way in range(2):
+            x_copy(0, way, n).wait_send()
+            x_copy(1, way, n).start()
         for way in range(2):
             x_copy(0, way, n).wait_recv()
             co_send[way, n] = (
@@ -299,24 +332,32 @@
             out_cps.append(cp)
     for cp in out_cps:
         cp.wait()
-    for j in range(NBITS):
-        for h in range(HEADS):
-            st_copy(j, h).wait_send()
+    for d in range(3):
+        @pl.when(z_sends(d))
+        def _():
+            for h in range(HEADS):
+                z_copy(d, h).wait_send()
+
+        @pl.when(y_id + 1 + d < 4)
+        def _():
+            for h in range(HEADS):
+                y_copy(d, h).wait_send()
     for o in range(4):
         for half in range(2):
             sib_copy(o, half).wait_send()
-    for kind in range(3):
+    for kind in (1, 2):
         for way in range(2):
             for n in range(NS):
                 x_copy(kind, way, n).wait_send()
 
 
 def per_device(tokens, w_query, w_key, w_value, w_out, norm_gain, level_weights, prior_states):
-    NS = 2
+    NS = 4
+    NF = len(FIRST)
     SUB = 256 // NS
     half = (2, NS, SUB, 512)
     scratch = [
-        pltpu.VMEM((NK, ROWS, KC), BF16),
+        pltpu.VMEM((ROWS, D), BF16),
         pltpu.VMEM((2, D, 256), BF16),
         pltpu.VMEM((2, D, 256), BF16),
         pltpu.VMEM((2, D, 256), BF16),
@@ -334,8 +375,10 @@
         pltpu.VMEM((HEADS, DH, DH), F32),
         pltpu.VMEM((HEADS, DH, ROWS), F32),
         pltpu.VMEM((ROWS, 512), BF16),
-        pltpu.VMEM((NBITS, HEADS, DH, DH), BF16),
-        pltpu.VMEM((NBITS, HEADS, DH, DH), BF16),
+        pltpu.VMEM((HEADS, DH, DH), BF16),
+        pltpu.VMEM((3, HEADS, DH, DH), BF16),
+        pltpu.VMEM((HEADS, DH, DH), BF16),
+        pltpu.VMEM((3, HEADS, DH, DH), BF16),
         pltpu.VMEM((4, 2, 256, 512), BF16),
         pltpu.VMEM((4, 2, 256, 512), BF16),
         pltpu.VMEM((4, 256, 512), F32),
@@ -346,13 +389,15 @@
         pltpu.VMEM(half, BF16),
         pltpu.VMEM(half, BF16),
         pltpu.VMEM(half, BF16),
-        pltpu.SemaphoreType.DMA((NK,)),
-        pltpu.SemaphoreType.DMA((3, 2, NK)),
+        pltpu.SemaphoreType.DMA((NF,)),
+        pltpu.SemaphoreType.DMA((3, 2, NF)),
         pltpu.SemaphoreType.DMA((8,)),
         pltpu.SemaphoreType.DMA((3,)),
         pltpu.SemaphoreType.DMA((2, NS)),
-        pltpu.SemaphoreType.DMA((NBITS, HEADS)),
-        pltpu.SemaphoreType.DMA((NBITS, HEADS)),
+        pltpu.SemaphoreType.DMA((3, HEADS)),
+        pltpu.SemaphoreType.DMA((3, HEADS)),
+        pltpu.SemaphoreType.DMA((3, HEADS)),
+        pltpu.SemaphoreType.DMA((3, HEADS)),
         pltpu.SemaphoreType.DMA((4, 2)),
         pltpu.SemaphoreType.DMA((4, 2)),
         pltpu.SemaphoreType.DMA((3, 2, NS)),

time: 57.6 us -> 51.7 us (0.90)
  the two profiles are of different devices: /device:TPU:1 before, /device:TPU:120 now
where the time goes in v2:
time: 51.7 us; the launch traced here: 51.5 us
  Pallas kernels  49.6 us (96%)
  local copies, waits for them, and re-layouts  1.87 us (4%)
    pallas_call x1, Pallas kernels, per_device(): pl.pallas_call(kernel, out_shape=jax.ShapeDtypeStruct((ROWS, 512), BF16),...  49.6 us
    unnamed x1, local copies, waits for them, and re-layouts  1.87 us

profile of v2, /device:TPU:120, one launch (start us, length us, event | category | flops | bytes accessed | tf_op | source)
XLA Modules:
  0.0 51.5 jit_solution(5551581136632698364)
XLA Ops:
  0.0 49.6 %shard_map.82 = bf16[512,512]{1,0:T(8,128)(2,1)} custom-call(bf16[512,4096]{1,0:T(8,128)(2,1)} %tok_hbm.1, bf16[4096,512]{1,0:T(8,128)(2,1)} %wq_hbm.1, bf16[4096,512]{1,0:T(8,128)(2,1)} %wk_hbm.1, bf16[4096,512]{1,0:T(8,128)(2,1)} %wv_hbm.1, bf16[512,4096]{1,0:T(8,128)(2,1)} %wo_hbm.1, f32[1,512]{1,0:T(1,128)} %bitcast.1, f32[21,4,512]{2,1,0:T(4,128)} %lam_hbm.1, ...), custom_call_target="tpu_custom_call" | custom-call | flops 9500000256 | bytes 22000000 | tf_op jit(solution)/shard_map/pallas_call | solution.py:406
  49.6 1.9 %copy.10 = bf16[512,512]{1,0:T(8,128)(2,1)} copy(bf16[512,512]{1,0:T(8,128)(2,1)} %shard_map.82) | data formatting | bytes 1048576

commit v3 on v2

v3 whole, which is shorter than its diff:
```python
import functools

import jax
import jax.numpy as jnp
from jax import lax
from jax.experimental import pallas as pl
from jax.experimental.pallas import tpu as pltpu
from jax.sharding import PartitionSpec as P

MESH = pl.DeviceIdType.MESH
F32 = jnp.float32
BF16 = jnp.bfloat16
eps = 1e-06

ROWS, D, HEADS, DH = 512, 4096, 4, 128
LEVELS, PRIOR = 21, 4
CH = 128
NC = ROWS // CH
SHIFT = 9


def pick(i, table):
    value = table[0]
    for n, entry in enumerate(table[1:], 1):
        if entry != table[n - 1]:
            value = jnp.where(i >= n, entry, value)
    return value


def dot(a, b):
    return jnp.dot(a, b, preferred_element_type=F32)


def kernel(
    tok_hbm, wq_hbm, wk_hbm, wv_hbm, wo_hbm, gain_hbm, lam_hbm, prior_hbm, out_hbm,
    tok, w, wo, gain, lam_raw, lam, prior,
    acc, k_s, vt_s, qt_s, chunk_st, state, y_s, normed,
    z_send, y_send, zy_recv, sib_send, sib_recv, csum, d2_recv, al_recv, co_send, co_recv, out_v,
    tok_sem, w_sem, wo_sem, misc_sem, out_sem, z_ss, y_ss, zy_rs, sib_ss, sib_rs, x_ss, x_rs,
):
    s_id = lax.axis_index("seq")
    h_id = lax.axis_index("head")
    x_id, c_id = h_id // 2, h_id % 2
    y_id, z_id = s_id // 4, s_id % 4
    sib = (s_id, x_id * 2 + (1 - c_id))
    right = (s_id, ((x_id + 1) % 4) * 2 + c_id)
    left = (s_id, ((x_id + 3) % 4) * 2 + c_id)

    zy_recv[...] = jnp.zeros_like(zy_recv)
    barrier = pltpu.get_barrier_semaphore()
    for dev in [sib, right, left]:
        pl.semaphore_signal(barrier, inc=1, device_id=dev, device_id_type=MESH)
    for d in range(1, 4):
        pl.semaphore_signal(barrier, inc=1, device_id=(y_id * 4 + (z_id + d) % 4, h_id), device_id_type=MESH)
        pl.semaphore_signal(barrier, inc=1, device_id=(((y_id + d) % 4) * 4 + z_id, h_id), device_id_type=MESH)

    TC = 1024

    def tok_cp(i):
        cols = pl.ds(i * TC, TC)
        return pltpu.make_async_copy(tok_hbm.at[:, cols], tok.at[:, cols], tok_sem.at[i])

    def w_cp(u):
        src = (wk_hbm, wv_hbm, wk_hbm, wv_hbm, wq_hbm, wq_hbm)[u]
        p = (0, 0, 1, 1, 0, 1)[u]
        return pltpu.make_async_copy(src.at[:, pl.ds(p * 256, 256)], w.at[u], w_sem.at[u])

    lam_cp = pltpu.make_async_copy(lam_hbm, lam_raw, misc_sem.at[0])
    prior_cp = pltpu.make_async_copy(prior_hbm, prior, misc_sem.at[1])
    gain_cp = pltpu.make_async_copy(gain_hbm, gain, misc_sem.at[2])
    wo_cp = [
        pltpu.make_async_copy(wo_hbm.at[:, pl.ds(b * 512, 512)], wo.at[b], wo_sem.at[b])
        for b in range(8)
    ]

    def z_copy(d, h):
        return pltpu.make_async_remote_copy(
            src_ref=z_send.at[h], dst_ref=zy_recv.at[h, :, pl.ds(d * DH, DH)],
            send_sem=z_ss.at[d, h], recv_sem=zy_rs.at[d, h],
            device_id=(y_id * 4 + (z_id + 1 + d) % 4, h_id), device_id_type=MESH,
        )

    def y_copy(d, h):
        return pltpu.make_async_remote_copy(
            src_ref=y_send.at[h], dst_ref=zy_recv.at[h, :, pl.ds((3 + d) * DH, DH)],
            send_sem=y_ss.at[d, h], recv_sem=zy_rs.at[3 + d, h],
            device_id=(((y_id + 1 + d) % 4) * 4 + z_id, h_id), device_id_type=MESH,
        )

    def z_sends(d):
        return (y_id < 3) | (z_id + 1 + d < 4)

    def z_comes(d):
        return (y_id < 3) | (z_id > d)

    def kv_post(p):
        for i in range(2):
            h = 2 * p + i
            raw = acc[2 * p, :, i * DH:(i + 1) * DH]
            k_s[h] = (raw * lax.rsqrt(jnp.sum(raw * raw, axis=-1, keepdims=True) + eps)).astype(BF16)
            vt_s[h] = acc[2 * p + 1, :, i * DH:(i + 1) * DH].T.astype(BF16)
            st = [
                dot(vt_s[h, :, c * CH:(c + 1) * CH], k_s[h, c * CH:(c + 1) * CH, :])
                for c in range(NC)
            ]
            s01 = st[0] + st[1]
            chunk_st[h, 0] = st[0].astype(BF16)
            chunk_st[h, 1] = s01.astype(BF16)
            chunk_st[h, 2] = st[2].astype(BF16)
            total = s01 + (st[2] + st[3])
            state[h] = total
            z_send[h] = total.astype(BF16)
            for d in range(3):
                @pl.when(z_sends(d))
                def _():
                    z_copy(d, h).start()

    def pass_on(h):
        for d in range(3):
            @pl.when(z_comes(d))
            def _():
                z_copy(d, h).wait_recv()

        @pl.when(y_id < 3)
        def _():
            got = [zy_recv[h, :, d * DH:(d + 1) * DH].astype(F32) for d in range(3)]
            y_send[h] = (state[h] + (got[0] + got[1] + got[2])).astype(BF16)
            for d in range(3):
                @pl.when(y_id + 1 + d < 4)
                def _():
                    y_copy(d, h).start()

    def q_post(p):
        for i in range(2):
            h = 2 * p + i
            raw = acc[4 + p, :, i * DH:(i + 1) * DH].T
            qt_s[h] = (raw * lax.rsqrt(jnp.sum(raw * raw, axis=0, keepdims=True) + eps)).astype(BF16)

    srow = lax.broadcasted_iota(jnp.int32, (CH, CH), 0)
    tcol = lax.broadcasted_iota(jnp.int32, (CH, CH), 1)

    def near(h):
        differ = srow ^ tcol
        level = jnp.zeros((CH, CH), jnp.int32)
        for bit in range(7):
            level = level + (differ >= (1 << bit)).astype(jnp.int32)
        level = jnp.where(srow <= tcol, level, 99)
        q_full = qt_s[h]
        qf = q_full.astype(F32)
        b_all = jnp.concatenate(
            [(lam[h, LEVELS - PRIOR + p:LEVELS - PRIOR + p + 1, :] * qf).astype(BF16) for p in range(PRIOR)], axis=0
        )
        a_all = jnp.concatenate([prior[p, h].T.astype(BF16) for p in range(PRIOR)], axis=1)
        y_s[h] = dot(a_all, b_all)
        l8 = (lam[h, 8:9, :] * qf).astype(BF16)
        l9 = (lam[h, 9:10, :] * qf).astype(BF16)
        for c in range(NC):
            cols = slice(c * CH, (c + 1) * CH)
            scores = dot(k_s[h, cols, :], q_full[:, cols])
            weight = jnp.zeros((CH, CH), F32)
            for lv in range(8):
                weight = jnp.where(level == lv, lam[h, lv:lv + 1, cols], weight)
            mix = (weight * scores).astype(BF16)
            y = dot(vt_s[h, :, cols], mix)
            if c % 2 == 1:
                y = y + dot(chunk_st[h, 0 if c == 1 else 2], l8[:, cols])
            if c >= 2:
                y = y + dot(chunk_st[h, 1], l9[:, cols])
            y_s[h, :, cols] += y

    def far_rows(at, level, h):
        odd = at % 2
        low, high = lam[h, level:level + 1, :], lam[h, level + 1:level + 2, :]
        first = odd.astype(F32) * low + jnp.where((odd == 0) & (at > 0), 1.0, 0.0) * high
        return [first] + [jnp.where(at > d, 1.0, 0.0) * high for d in (1, 2)]

    def finish(h):
        qf = qt_s[h].astype(F32)
        rows = far_rows(z_id, SHIFT + 1, h) + far_rows(y_id, SHIFT + 3, h)
        b_all = jnp.concatenate([(row * qf).astype(BF16) for row in rows], axis=0)
        for d in range(3):
            @pl.when(y_id > d)
            def _():
                y_copy(d, h).wait_recv()
        y = y_s[h] + dot(zy_recv[h], b_all)
        scale = lax.rsqrt(jnp.sum(y * y, axis=0, keepdims=True) * (1.0 / DH) + eps)
        cols = pl.ds(pl.multiple_of(h * DH, DH), DH)
        normed[:, cols] = ((y * scale).T * gain[0:1, cols]).astype(BF16)

    for i in range(D // TC):
        tok_cp(i).start()
    w_cp(0).start()
    w_cp(1).start()
    for i in range(D // TC):
        tok_cp(i).wait()

    def unit(u, _):
        @pl.when(u == 0)
        def _():
            w_cp(2).start()
            w_cp(3).start()

        @pl.when(u == 1)
        def _():
            w_cp(4).start()
            w_cp(5).start()

        @pl.when(u == 2)
        def _():
            lam_cp.start()
            prior_cp.start()
            gain_cp.start()
            for b in range(8):
                wo_cp[b].start()

        pltpu.make_async_copy(wk_hbm.at[:, pl.ds(0, 256)], w.at[u], w_sem.at[u]).wait()
        acc[u] = dot(tok[...], w[u])

        @pl.when(u == 1)
        def _():
            pl.semaphore_wait(barrier, 9)

        @pl.when((u == 1) | (u == 3))
        def _():
            kv_post(u // 2)

        @pl.when(u >= 4)
        def _():
            q_post(u - 4)
        return 0

    lax.fori_loop(0, 6, unit, 0)
    lam_cp.wait()
    prior_cp.wait()
    gain_cp.wait()
    for h in range(HEADS):
        lam[h] = lam_raw[:, h, :]

    def near_step(h, _):
        near(h)
        pass_on(h)
        return 0

    lax.fori_loop(0, HEADS, near_step, 0)

    def finish_step(h, _):
        finish(h)
        return 0

    lax.fori_loop(0, HEADS, finish_step, 0)
    for b in range(8):
        wo_cp[b].wait()

    HALF = 256
    NS = co_send.shape[1]
    SUB = HALF // NS

    def sib_copy(o, half):
        return pltpu.make_async_remote_copy(
            src_ref=sib_send.at[o, half], dst_ref=sib_recv.at[o, half],
            send_sem=sib_ss.at[o, half], recv_sem=sib_rs.at[o, half],
            device_id=sib, device_id_type=MESH,
        )

    def x_copy(kind, way, n):
        rows = pl.ds(pl.multiple_of(n * SUB, SUB), SUB)
        o = 1 if way == 0 else 3
        src = (csum.at[2, way, rows], csum.at[o, 1 - way, rows], co_send.at[way, n])[kind]
        dst = (d2_recv, al_recv, co_recv)[kind]
        return pltpu.make_async_remote_copy(
            src_ref=src, dst_ref=dst.at[way, n],
            send_sem=x_ss.at[kind, way, n], recv_sem=x_rs.at[kind, way, n],
            device_id=right if way == 0 else left, device_id_type=MESH,
        )

    order = (
        (0, 2, 0), (0, 2, 1), (0, 1, 1), (0, 3, 0), (1, 2, 0), (1, 2, 1), (0, 1, 0), (0, 3, 1),
        (1, 1, 1), (1, 3, 0), (0, 0, 0), (0, 0, 1), (1, 1, 0), (1, 3, 1), (1, 0, 0), (1, 0, 1),
    )

    def out_step(i, _):
        kind, o, half = (pick(i, [step[n] for step in order]) for n in range(3))
        column = ((x_id + o) % 4) * 2 + jnp.where(kind == 0, 1 - c_id, c_id)
        part = dot(normed[pl.ds(pl.multiple_of(half * HALF, HALF), HALF), :], wo[column])

        @pl.when(kind == 0)
        def _():
            sib_send[o, half] = part.astype(BF16)
            sib_copy(o, half).start()

        @pl.when(kind == 1)
        def _():
            sib_copy(o, half).wait_recv()
            csum[o, half] = (part + sib_recv[o, half].astype(F32)).astype(BF16)

        for way in range(2):
            @pl.when((kind == 1) & (o == 2) & (half == way))
            def _():
                for n in range(NS):
                    x_copy(0, way, n).start()
        return 0

    lax.fori_loop(0, 16, out_step, 0)

    def x_step(n, _):
        rows = pl.ds(pl.multiple_of(n * SUB, SUB), SUB)
        for way in range(2):
            x_copy(0, way, n).wait_send()
            x_copy(1, way, n).start()
        for way in range(2):
            x_copy(0, way, n).wait_recv()
            co_send[way, n] = (
                csum[1 if way == 0 else 3, way, rows, :].astype(F32) + d2_recv[way, n].astype(F32)
            ).astype(BF16)
            x_copy(2, way, n).start()
        return 0

    lax.fori_loop(0, NS, x_step, 0)

    def out_cp(half, n):
        rows = pl.ds(pl.multiple_of(half * HALF + n * SUB, SUB), SUB)
        return pltpu.make_async_copy(out_v.at[half, n], out_hbm.at[rows, :], out_sem.at[half, n])

    def last_step(n, _):
        rows = pl.ds(pl.multiple_of(n * SUB, SUB), SUB)
        for half in range(2):
            x_copy(1, 1 - half, n).wait_recv()
            x_copy(2, half, n).wait_recv()
            out_v[half, n] = (
                csum[0, half, rows, :].astype(F32) + al_recv[1 - half, n].astype(F32) + co_recv[half, n].astype(F32)
            ).astype(BF16)
            out_cp(half, n).start()
        return 0

    lax.fori_loop(0, NS, last_step, 0)

    def drain_x(n, _):
        for way in range(2):
            for kind in (1, 2):
                x_copy(kind, way, n).wait_send()
            out_cp(way, n).wait()
        return 0

    lax.fori_loop(0, NS, drain_x, 0)

    def drain(i, _):
        for d in range(3):
            @pl.when(z_sends(d))
            def _():
                z_copy(d, i).wait_send()

            @pl.when(y_id + 1 + d < 4)
            def _():
                y_copy(d, i).wait_send()
        for half in range(2):
            sib_copy(i, half).wait_send()
        return 0

    lax.fori_loop(0, HEADS, drain, 0)


def per_device(tokens, w_query, w_key, w_value, w_out, norm_gain, level_weights, prior_states):
    NS = 4
    SUB = 256 // NS
    half = (2, NS, SUB, 512)
    scratch = [
        pltpu.VMEM((ROWS, D), BF16),
        pltpu.VMEM((6, D, 256), BF16),
        pltpu.VMEM((8, 512, 512), BF16),
        pltpu.VMEM((1, 512), F32),
        pltpu.VMEM((LEVELS, HEADS, ROWS), F32),
        pltpu.VMEM((HEADS, LEVELS, ROWS), F32),
        pltpu.VMEM((PRIOR, HEADS, DH, DH), F32),
        pltpu.VMEM((6, ROWS, 256), F32),
        pltpu.VMEM((HEADS, ROWS, DH), BF16),
        pltpu.VMEM((HEADS, DH, ROWS), BF16),
        pltpu.VMEM((HEADS, DH, ROWS), BF16),
        pltpu.VMEM((HEADS, 3, DH, DH), BF16),
        pltpu.VMEM((HEADS, DH, DH), F32),
        pltpu.VMEM((HEADS, DH, ROWS), F32),
        pltpu.VMEM((ROWS, 512), BF16),
        pltpu.VMEM((HEADS, DH, DH), BF16),
        pltpu.VMEM((HEADS, DH, DH), BF16),
        pltpu.VMEM((HEADS, DH, 6 * DH), BF16),
        pltpu.VMEM((4, 2, 256, 512), BF16),
        pltpu.VMEM((4, 2, 256, 512), BF16),
        pltpu.VMEM((4, 2, 256, 512), BF16),
        pltpu.VMEM(half, BF16),
        pltpu.VMEM(half, BF16),
        pltpu.VMEM(half, BF16),
        pltpu.VMEM(half, BF16),
        pltpu.VMEM(half, BF16),
        pltpu.SemaphoreType.DMA((4,)),
        pltpu.SemaphoreType.DMA((6,)),
        pltpu.SemaphoreType.DMA((8,)),
        pltpu.SemaphoreType.DMA((3,)),
        pltpu.SemaphoreType.DMA((2, NS)),
        pltpu.SemaphoreType.DMA((3, HEADS)),
        pltpu.SemaphoreType.DMA((3, HEADS)),
        pltpu.SemaphoreType.DMA((6, HEADS)),
        pltpu.SemaphoreType.DMA((4, 2)),
        pltpu.SemaphoreType.DMA((4, 2)),
        pltpu.SemaphoreType.DMA((3, 2, NS)),
        pltpu.SemaphoreType.DMA((3, 2, NS)),
    ]
    return pl.pallas_call(
        kernel,
        out_shape=jax.ShapeDtypeStruct((ROWS, 512), BF16),
        in_specs=[pl.BlockSpec(memory_space=pl.ANY)] * 8,
        out_specs=pl.BlockSpec(memory_space=pl.ANY),
        scratch_shapes=scratch,
        compiler_params=pltpu.CompilerParams(
            collective_id=0, has_side_effects=True, vmem_limit_bytes=58 << 20
        ),
        cost_estimate=pl.CostEstimate(flops=9_500_000_000, bytes_accessed=22_000_000, transcendentals=0),
    )(tokens, w_query, w_key, w_value, w_out, norm_gain.reshape(1, 512), level_weights, prior_states)


def solution(mesh):
    placed = (
        P("seq", None),
        P(None, "head"),
        P(None, "head"),
        P(None, "head"),
        P("head", None),
        P("head"),
        P(None, "head", "seq"),
        P(None, "head", None, None),
    )
    return jax.shard_map(
        per_device, mesh=mesh, in_specs=placed, out_specs=P("seq", "head"), check_vma=False
    )
```

time: 51.7 us -> 47.6 us (0.921)
  the two profiles are of different devices: /device:TPU:120 before, /device:TPU:24 now
where the time goes in v3:
time: 47.6 us; the launch traced here: 47.4 us
  Pallas kernels  45.6 us (96%)
  local copies, waits for them, and re-layouts  1.87 us (4%)
    pallas_call x1, Pallas kernels, per_device(): pl.pallas_call(kernel, out_shape=jax.ShapeDtypeStruct((ROWS, 512), BF16),...  45.6 us
    unnamed x1, local copies, waits for them, and re-layouts  1.87 us

profile of v3, /device:TPU:24, one launch (start us, length us, event | category | flops | bytes accessed | tf_op | source)
XLA Modules:
  0.0 47.4 jit_solution(777901299813961267)
XLA Ops:
  0.0 45.6 %shard_map.82 = bf16[512,512]{1,0:T(8,128)(2,1)} custom-call(bf16[512,4096]{1,0:T(8,128)(2,1)} %tok_hbm.1, bf16[4096,512]{1,0:T(8,128)(2,1)} %wq_hbm.1, bf16[4096,512]{1,0:T(8,128)(2,1)} %wk_hbm.1, bf16[4096,512]{1,0:T(8,128)(2,1)} %wv_hbm.1, bf16[512,4096]{1,0:T(8,128)(2,1)} %wo_hbm.1, f32[1,512]{1,0:T(1,128)} %bitcast.1, f32[21,4,512]{2,1,0:T(4,128)} %lam_hbm.1, ...), custom_call_target="tpu_custom_call" | custom-call | flops 9500000256 | bytes 22000000 | tf_op jit(solution)/shard_map/pallas_call | solution.py:406
  45.6 1.9 %copy.10 = bf16[512,512]{1,0:T(8,128)(2,1)} copy(bf16[512,512]{1,0:T(8,128)(2,1)} %shard_map.82) | data formatting | bytes 1048576

commit v4 on v3

--- a/solution.py
+++ b/solution.py
@@ -151,7 +151,8 @@
             [(lam[h, LEVELS - PRIOR + p:LEVELS - PRIOR + p + 1, :] * qf).astype(BF16) for p in range(PRIOR)], axis=0
         )
         a_all = jnp.concatenate([prior[p, h].T.astype(BF16) for p in range(PRIOR)], axis=1)
-        y_s[h] = dot(a_all, b_all)
+        base = dot(a_all, b_all)
+        parts = []
         l8 = (lam[h, 8:9, :] * qf).astype(BF16)
         l9 = (lam[h, 9:10, :] * qf).astype(BF16)
         for c in range(NC):
@@ -166,26 +167,24 @@
                 y = y + dot(chunk_st[h, 0 if c == 1 else 2], l8[:, cols])
             if c >= 2:
                 y = y + dot(chunk_st[h, 1], l9[:, cols])
-            y_s[h, :, cols] += y
-
-    def far_rows(at, level, h):
+            parts.append(y)
+        y_s[h] = base + jnp.concatenate(parts, axis=1)
+
+    def far_rows(at, level, h, toks):
         odd = at % 2
-        low, high = lam[h, level:level + 1, :], lam[h, level + 1:level + 2, :]
+        low, high = lam[h, level:level + 1, toks], lam[h, level + 1:level + 2, toks]
         first = odd.astype(F32) * low + jnp.where((odd == 0) & (at > 0), 1.0, 0.0) * high
         return [first] + [jnp.where(at > d, 1.0, 0.0) * high for d in (1, 2)]
 
-    def finish(h):
-        qf = qt_s[h].astype(F32)
-        rows = far_rows(z_id, SHIFT + 1, h) + far_rows(y_id, SHIFT + 3, h)
+    def finish(h, part):
+        toks = pl.ds(pl.multiple_of(part * 256, 256), 256)
+        qf = qt_s[h, :, toks].astype(F32)
+        rows = far_rows(z_id, SHIFT + 1, h, toks) + far_rows(y_id, SHIFT + 3, h, toks)
         b_all = jnp.concatenate([(row * qf).astype(BF16) for row in rows], axis=0)
-        for d in range(3):
-            @pl.when(y_id > d)
-            def _():
-                y_copy(d, h).wait_recv()
-        y = y_s[h] + dot(zy_recv[h], b_all)
+        y = y_s[h, :, toks] + dot(zy_recv[h], b_all)
         scale = lax.rsqrt(jnp.sum(y * y, axis=0, keepdims=True) * (1.0 / DH) + eps)
         cols = pl.ds(pl.multiple_of(h * DH, DH), DH)
-        normed[:, cols] = ((y * scale).T * gain[0:1, cols]).astype(BF16)
+        normed[toks, cols] = ((y * scale).T * gain[0:1, cols]).astype(BF16)
 
     for i in range(D // TC):
         tok_cp(i).start()
@@ -227,6 +226,7 @@
         @pl.when(u >= 4)
         def _():
             q_post(u - 4)
+            pass_on(u - 4)
         return 0
 
     lax.fori_loop(0, 6, unit, 0)
@@ -236,36 +236,34 @@
     for h in range(HEADS):
         lam[h] = lam_raw[:, h, :]
 
-    def near_step(h, _):
-        near(h)
-        pass_on(h)
-        return 0
-
-    lax.fori_loop(0, HEADS, near_step, 0)
-
-    def finish_step(h, _):
-        finish(h)
-        return 0
-
-    lax.fori_loop(0, HEADS, finish_step, 0)
+    def near_step(i, _):
+        near(2 * i)
+        near(2 * i + 1)
+
+        @pl.when(i == 0)
+        def _():
+            pass_on(2)
+            pass_on(3)
+        return 0
+
+    lax.fori_loop(0, 2, near_step, 0)
     for b in range(8):
         wo_cp[b].wait()
 
-    HALF = 256
     NS = co_send.shape[1]
-    SUB = HALF // NS
-
-    def sib_copy(o, half):
+    SUB = ROWS // NS
+    W = 256
+
+    def sib_copy(o, n):
         return pltpu.make_async_remote_copy(
-            src_ref=sib_send.at[o, half], dst_ref=sib_recv.at[o, half],
-            send_sem=sib_ss.at[o, half], recv_sem=sib_rs.at[o, half],
+            src_ref=sib_send.at[o, n], dst_ref=sib_recv.at[o, n],
+            send_sem=sib_ss.at[o, n], recv_sem=sib_rs.at[o, n],
             device_id=sib, device_id_type=MESH,
         )
 
     def x_copy(kind, way, n):
-        rows = pl.ds(pl.multiple_of(n * SUB, SUB), SUB)
         o = 1 if way == 0 else 3
-        src = (csum.at[2, way, rows], csum.at[o, 1 - way, rows], co_send.at[way, n])[kind]
+        src = (csum.at[2, n, way], csum.at[o, n, 1 - way], co_send.at[way, n])[kind]
         dst = (d2_recv, al_recv, co_recv)[kind]
         return pltpu.make_async_remote_copy(
             src_ref=src, dst_ref=dst.at[way, n],
@@ -273,72 +271,102 @@
             device_id=right if way == 0 else left, device_id_type=MESH,
         )
 
-    order = (
-        (0, 2, 0), (0, 2, 1), (0, 1, 1), (0, 3, 0), (1, 2, 0), (1, 2, 1), (0, 1, 0), (0, 3, 1),
-        (1, 1, 1), (1, 3, 0), (0, 0, 0), (0, 0, 1), (1, 1, 0), (1, 3, 1), (1, 0, 0), (1, 0, 1),
-    )
-
-    def out_step(i, _):
-        kind, o, half = (pick(i, [step[n] for step in order]) for n in range(3))
-        column = ((x_id + o) % 4) * 2 + jnp.where(kind == 0, 1 - c_id, c_id)
-        part = dot(normed[pl.ds(pl.multiple_of(half * HALF, HALF), HALF), :], wo[column])
-
-        @pl.when(kind == 0)
-        def _():
-            sib_send[o, half] = part.astype(BF16)
-            sib_copy(o, half).start()
-
-        @pl.when(kind == 1)
-        def _():
-            sib_copy(o, half).wait_recv()
-            csum[o, half] = (part + sib_recv[o, half].astype(F32)).astype(BF16)
-
+    def rows_of(n):
+        return pl.ds(pl.multiple_of(n * SUB, SUB), SUB)
+
+    def for_sib(n):
+        def step(i, _):
+            o = pick(i, (2, 1, 3, 0))
+            sib_send[o, n] = dot(normed[rows_of(n), :], wo[((x_id + o) % 4) * 2 + 1 - c_id]).astype(BF16)
+            sib_copy(o, n).start()
+            return 0
+
+        lax.fori_loop(0, 4, step, 0)
+
+    def chip_sum(n):
+        def step(i, _):
+            o = pick(i, (2, 1, 3, 0))
+            part = dot(normed[rows_of(n), :], wo[((x_id + o) % 4) * 2 + c_id])
+            sib_copy(o, n).wait_recv()
+            total = (part + sib_recv[o, n].astype(F32)).astype(BF16)
+            csum[o, n, 0] = total[:, :W]
+            csum[o, n, 1] = total[:, W:]
+
+            @pl.when(i == 0)
+            def _():
+                for way in range(2):
+                    x_copy(0, way, n).start()
+            return 0
+
+        lax.fori_loop(0, 4, step, 0)
         for way in range(2):
-            @pl.when((kind == 1) & (o == 2) & (half == way))
-            def _():
-                for n in range(NS):
-                    x_copy(0, way, n).start()
-        return 0
-
-    lax.fori_loop(0, 16, out_step, 0)
+            x_copy(1, way, n).start()
+
+    def stage(n, _):
+        @pl.when(n % 2 == 0)
+        def _():
+            @pl.when(n == 0)
+            def _():
+                def wait_y(h, _):
+                    for d in range(3):
+                        @pl.when(y_id > d)
+                        def _():
+                            y_copy(d, h).wait_recv()
+                    return 0
+
+                lax.fori_loop(0, HEADS, wait_y, 0)
+
+            @pl.when(n < NS)
+            def _():
+                def two(i, _):
+                    finish(2 * i, n // 2)
+                    finish(2 * i + 1, n // 2)
+                    return 0
+
+                lax.fori_loop(0, 2, two, 0)
+
+        @pl.when(n < NS)
+        def _():
+            for_sib(n)
+
+        @pl.when(n > 0)
+        def _():
+            chip_sum(n - 1)
+        return 0
+
+    lax.fori_loop(0, NS + 1, stage, 0)
 
     def x_step(n, _):
-        rows = pl.ds(pl.multiple_of(n * SUB, SUB), SUB)
-        for way in range(2):
-            x_copy(0, way, n).wait_send()
-            x_copy(1, way, n).start()
         for way in range(2):
             x_copy(0, way, n).wait_recv()
             co_send[way, n] = (
-                csum[1 if way == 0 else 3, way, rows, :].astype(F32) + d2_recv[way, n].astype(F32)
+                csum[1 if way == 0 else 3, n, way].astype(F32) + d2_recv[way, n].astype(F32)
             ).astype(BF16)
             x_copy(2, way, n).start()
         return 0
 
     lax.fori_loop(0, NS, x_step, 0)
 
-    def out_cp(half, n):
-        rows = pl.ds(pl.multiple_of(half * HALF + n * SUB, SUB), SUB)
-        return pltpu.make_async_copy(out_v.at[half, n], out_hbm.at[rows, :], out_sem.at[half, n])
+    def out_cp(n):
+        return pltpu.make_async_copy(out_v.at[n], out_hbm.at[rows_of(n), :], out_sem.at[n])
 
     def last_step(n, _):
-        rows = pl.ds(pl.multiple_of(n * SUB, SUB), SUB)
         for half in range(2):
             x_copy(1, 1 - half, n).wait_recv()
             x_copy(2, half, n).wait_recv()
-            out_v[half, n] = (
-                csum[0, half, rows, :].astype(F32) + al_recv[1 - half, n].astype(F32) + co_recv[half, n].astype(F32)
+            out_v[n, :, half * W:(half + 1) * W] = (
+                csum[0, n, half].astype(F32) + al_recv[1 - half, n].astype(F32) + co_recv[half, n].astype(F32)
             ).astype(BF16)
-            out_cp(half, n).start()
+        out_cp(n).start()
         return 0
 
     lax.fori_loop(0, NS, last_step, 0)
 
     def drain_x(n, _):
         for way in range(2):
-            for kind in (1, 2):
+            for kind in range(3):
                 x_copy(kind, way, n).wait_send()
-            out_cp(way, n).wait()
+        out_cp(n).wait()
         return 0
 
     lax.fori_loop(0, NS, drain_x, 0)
@@ -352,8 +380,8 @@
             @pl.when(y_id + 1 + d < 4)
             def _():
                 y_copy(d, i).wait_send()
-        for half in range(2):
-            sib_copy(i, half).wait_send()
+        for n in range(NS):
+            sib_copy(i, n).wait_send()
         return 0
 
     lax.fori_loop(0, HEADS, drain, 0)
@@ -361,8 +389,8 @@
 
 def per_device(tokens, w_query, w_key, w_value, w_out, norm_gain, level_weights, prior_states):
     NS = 4
-    SUB = 256 // NS
-    half = (2, NS, SUB, 512)
+    SUB = ROWS // NS
+    half = (2, NS, SUB, 256)
     scratch = [
         pltpu.VMEM((ROWS, D), BF16),
         pltpu.VMEM((6, D, 256), BF16),
@@ -382,24 +410,24 @@
         pltpu.VMEM((HEADS, DH, DH), BF16),
         pltpu.VMEM((HEADS, DH, DH), BF16),
         pltpu.VMEM((HEADS, DH, 6 * DH), BF16),
-        pltpu.VMEM((4, 2, 256, 512), BF16),
-        pltpu.VMEM((4, 2, 256, 512), BF16),
-        pltpu.VMEM((4, 2, 256, 512), BF16),
+        pltpu.VMEM((4, NS, SUB, 512), BF16),
+        pltpu.VMEM((4, NS, SUB, 512), BF16),
+        pltpu.VMEM((4, NS, 2, SUB, 256), BF16),
         pltpu.VMEM(half, BF16),
         pltpu.VMEM(half, BF16),
         pltpu.VMEM(half, BF16),
         pltpu.VMEM(half, BF16),
-        pltpu.VMEM(half, BF16),
+        pltpu.VMEM((NS, SUB, 512), BF16),
         pltpu.SemaphoreType.DMA((4,)),
         pltpu.SemaphoreType.DMA((6,)),
         pltpu.SemaphoreType.DMA((8,)),
         pltpu.SemaphoreType.DMA((3,)),
-        pltpu.SemaphoreType.DMA((2, NS)),
+        pltpu.SemaphoreType.DMA((NS,)),
         pltpu.SemaphoreType.DMA((3, HEADS)),
         pltpu.SemaphoreType.DMA((3, HEADS)),
         pltpu.SemaphoreType.DMA((6, HEADS)),
-        pltpu.SemaphoreType.DMA((4, 2)),
-        pltpu.SemaphoreType.DMA((4, 2)),
+        pltpu.SemaphoreType.DMA((4, NS)),
+        pltpu.SemaphoreType.DMA((4, NS)),
         pltpu.SemaphoreType.DMA((3, 2, NS)),
         pltpu.SemaphoreType.DMA((3, 2, NS)),
     ]

time: 47.6 us -> 47.7 us (level)
  no operation moved by 1% of the time
where the time goes in v4:
time: 47.7 us; the launch traced here: 47.6 us
  Pallas kernels  45.7 us (96%)
  local copies, waits for them, and re-layouts  1.87 us (4%)
    pallas_call x1, Pallas kernels, per_device(): pl.pallas_call(kernel, out_shape=jax.ShapeDtypeStruct((ROWS, 512), BF16),...  45.7 us
    unnamed x1, local copies, waits for them, and re-layouts  1.87 us

profile of v4, /device:TPU:24, one launch (start us, length us, event | category | flops | bytes accessed | tf_op | source)
XLA Modules:
  0.0 47.6 jit_solution(2618579025953538053)
XLA Ops:
  0.0 45.7 %shard_map.82 = bf16[512,512]{1,0:T(8,128)(2,1)} custom-call(bf16[512,4096]{1,0:T(8,128)(2,1)} %tok_hbm.1, bf16[4096,512]{1,0:T(8,128)(2,1)} %wq_hbm.1, bf16[4096,512]{1,0:T(8,128)(2,1)} %wk_hbm.1, bf16[4096,512]{1,0:T(8,128)(2,1)} %wv_hbm.1, bf16[512,4096]{1,0:T(8,128)(2,1)} %wo_hbm.1, f32[1,512]{1,0:T(1,128)} %bitcast.1, f32[21,4,512]{2,1,0:T(4,128)} %lam_hbm.1, ...), custom_call_target="tpu_custom_call" | custom-call | flops 9500000256 | bytes 22000000 | tf_op jit(solution)/shard_map/pallas_call | solution.py:434
  45.7 1.9 %copy.10 = bf16[512,512]{1,0:T(8,128)(2,1)} copy(bf16[512,512]{1,0:T(8,128)(2,1)} %shard_map.82) | data formatting | bytes 1048576

commit v5 on v4

--- a/solution.py
+++ b/solution.py
@@ -35,8 +35,8 @@
     tok_hbm, wq_hbm, wk_hbm, wv_hbm, wo_hbm, gain_hbm, lam_hbm, prior_hbm, out_hbm,
     tok, w, wo, gain, lam_raw, lam, prior,
     acc, k_s, vt_s, qt_s, chunk_st, state, y_s, normed,
-    z_send, y_send, zy_recv, sib_send, sib_recv, csum, d2_recv, al_recv, co_send, co_recv, out_v,
-    tok_sem, w_sem, wo_sem, misc_sem, out_sem, z_ss, y_ss, zy_rs, sib_ss, sib_rs, x_ss, x_rs,
+    z_send, y_send, zy_recv, sib_send, sib_recv, own_p, csum, d2_recv, al_recv, co_send, co_recv, out_v,
+    tok_sem, first_sem, w_sem, wo_sem, misc_sem, out_sem, z_ss, y_ss, zy_rs, sib_ss, sib_rs, x_ss, x_rs,
 ):
     s_id = lax.axis_index("seq")
     h_id = lax.axis_index("head")
@@ -186,29 +186,38 @@
         cols = pl.ds(pl.multiple_of(h * DH, DH), DH)
         normed[toks, cols] = ((y * scale).T * gain[0:1, cols]).astype(BF16)
 
+    def first_cp(k):
+        rows = pl.ds(pl.multiple_of(k * TC, TC), TC)
+        return pltpu.make_async_copy(wk_hbm.at[rows, pl.ds(0, 256)], w.at[0, rows, :], first_sem.at[k])
+
     for i in range(D // TC):
         tok_cp(i).start()
-    w_cp(0).start()
+        first_cp(i).start()
     w_cp(1).start()
-    for i in range(D // TC):
-        tok_cp(i).wait()
+    acc[0] = jnp.zeros((ROWS, 256), F32)
+
+    def first_unit(k, _):
+        part = pl.ds(pl.multiple_of(k * TC, TC), TC)
+        pltpu.make_async_copy(tok_hbm.at[:, part], tok.at[:, part], tok_sem.at[k]).wait()
+        first_cp(k).wait()
+        acc[0] += dot(tok[:, part], w[0, part, :])
+        return 0
+
+    lax.fori_loop(0, D // TC, first_unit, 0)
+    w_cp(2).start()
+    w_cp(3).start()
 
     def unit(u, _):
-        @pl.when(u == 0)
-        def _():
-            w_cp(2).start()
-            w_cp(3).start()
-
-        @pl.when(u == 1)
+        @pl.when(u == 2)
         def _():
             w_cp(4).start()
             w_cp(5).start()
-
-        @pl.when(u == 2)
-        def _():
             lam_cp.start()
             prior_cp.start()
             gain_cp.start()
+
+        @pl.when(u == 3)
+        def _():
             for b in range(8):
                 wo_cp[b].start()
 
@@ -229,7 +238,7 @@
             pass_on(u - 4)
         return 0
 
-    lax.fori_loop(0, 6, unit, 0)
+    lax.fori_loop(1, 6, unit, 0)
     lam_cp.wait()
     prior_cp.wait()
     gain_cp.wait()
@@ -240,11 +249,16 @@
         near(2 * i)
         near(2 * i + 1)
 
-        @pl.when(i == 0)
+        @pl.when((i == 0) & (z_id == 0))
         def _():
             pass_on(2)
             pass_on(3)
         return 0
+
+    @pl.when(z_id > 0)
+    def _():
+        pass_on(2)
+        pass_on(3)
 
     lax.fori_loop(0, 2, near_step, 0)
     for b in range(8):
@@ -274,33 +288,25 @@
     def rows_of(n):
         return pl.ds(pl.multiple_of(n * SUB, SUB), SUB)
 
-    def for_sib(n):
-        def step(i, _):
-            o = pick(i, (2, 1, 3, 0))
-            sib_send[o, n] = dot(normed[rows_of(n), :], wo[((x_id + o) % 4) * 2 + 1 - c_id]).astype(BF16)
+    def project_out(n):
+        here = normed[rows_of(n), :]
+        for o in (2, 1, 3, 0):
+            sib_send[o, n] = dot(here, wo[((x_id + o) % 4) * 2 + 1 - c_id]).astype(BF16)
+            own_p[o, n] = dot(here, wo[((x_id + o) % 4) * 2 + c_id])
+        for o in (2, 1, 3, 0):
             sib_copy(o, n).start()
-            return 0
-
-        lax.fori_loop(0, 4, step, 0)
 
     def chip_sum(n):
-        def step(i, _):
-            o = pick(i, (2, 1, 3, 0))
-            part = dot(normed[rows_of(n), :], wo[((x_id + o) % 4) * 2 + c_id])
+        for o in (2, 1, 3, 0):
             sib_copy(o, n).wait_recv()
-            total = (part + sib_recv[o, n].astype(F32)).astype(BF16)
+            total = (own_p[o, n] + sib_recv[o, n].astype(F32)).astype(BF16)
             csum[o, n, 0] = total[:, :W]
             csum[o, n, 1] = total[:, W:]
-
-            @pl.when(i == 0)
-            def _():
+            if o == 2:
                 for way in range(2):
                     x_copy(0, way, n).start()
-            return 0
-
-        lax.fori_loop(0, 4, step, 0)
-        for way in range(2):
-            x_copy(1, way, n).start()
+            elif o != 0:
+                x_copy(1, 0 if o == 1 else 1, n).start()
 
     def stage(n, _):
         @pl.when(n % 2 == 0)
@@ -327,7 +333,7 @@
 
         @pl.when(n < NS)
         def _():
-            for_sib(n)
+            project_out(n)
 
         @pl.when(n > 0)
         def _():
@@ -412,12 +418,14 @@
         pltpu.VMEM((HEADS, DH, 6 * DH), BF16),
         pltpu.VMEM((4, NS, SUB, 512), BF16),
         pltpu.VMEM((4, NS, SUB, 512), BF16),
+        pltpu.VMEM((4, NS, SUB, 512), F32),
         pltpu.VMEM((4, NS, 2, SUB, 256), BF16),
         pltpu.VMEM(half, BF16),
         pltpu.VMEM(half, BF16),
         pltpu.VMEM(half, BF16),
         pltpu.VMEM(half, BF16),
         pltpu.VMEM((NS, SUB, 512), BF16),
+        pltpu.SemaphoreType.DMA((4,)),
         pltpu.SemaphoreType.DMA((4,)),
         pltpu.SemaphoreType.DMA((6,)),
         pltpu.SemaphoreType.DMA((8,)),

time: 47.7 us -> 47.2 us (0.990)
  Pallas kernels: 45.7 us -> 45.1 us
    pallas_call x1, Pallas kernels: 45.7 us -> 45.1 us  [per_device(): pl.pallas_call(kernel, out_shape=jax.ShapeDtypeStruct((ROWS, 512), BF16),...]
where the time goes in v5:
time: 47.2 us; the launch traced here: 47 us
  Pallas kernels  45.1 us (96%)
  local copies, waits for them, and re-layouts  1.87 us (4%)
    pallas_call x1, Pallas kernels, per_device(): pl.pallas_call(kernel, out_shape=jax.ShapeDtypeStruct((ROWS, 512), BF16),...  45.1 us
    unnamed x1, local copies, waits for them, and re-layouts  1.87 us

profile of v5, /device:TPU:24, one launch (start us, length us, event | category | flops | bytes accessed | tf_op | source)
XLA Modules:
  0.0 47.0 jit_solution(11162357182576623919)
XLA Ops:
  0.0 45.1 %shard_map.82 = bf16[512,512]{1,0:T(8,128)(2,1)} custom-call(bf16[512,4096]{1,0:T(8,128)(2,1)} %tok_hbm.1, bf16[4096,512]{1,0:T(8,128)(2,1)} %wq_hbm.1, bf16[4096,512]{1,0:T(8,128)(2,1)} %wk_hbm.1, bf16[4096,512]{1,0:T(8,128)(2,1)} %wv_hbm.1, bf16[512,4096]{1,0:T(8,128)(2,1)} %wo_hbm.1, f32[1,512]{1,0:T(1,128)} %bitcast.1, f32[21,4,512]{2,1,0:T(4,128)} %lam_hbm.1, ...), custom_call_target="tpu_custom_call" | custom-call | flops 9500000256 | bytes 22000000 | tf_op jit(solution)/shard_map/pallas_call | solution.py:442
  45.1 1.9 %copy.10 = bf16[512,512]{1,0:T(8,128)(2,1)} copy(bf16[512,512]{1,0:T(8,128)(2,1)} %shard_map.82) | data formatting | bytes 1048576

commit v6 on v5

--- a/solution.py
+++ b/solution.py
@@ -61,9 +61,16 @@
         return pltpu.make_async_copy(tok_hbm.at[:, cols], tok.at[:, cols], tok_sem.at[i])
 
     def w_cp(u):
-        src = (wk_hbm, wv_hbm, wk_hbm, wv_hbm, wq_hbm, wq_hbm)[u]
-        p = (0, 0, 1, 1, 0, 1)[u]
-        return pltpu.make_async_copy(src.at[:, pl.ds(p * 256, 256)], w.at[u], w_sem.at[u])
+        if u >= 4:
+            return [pltpu.make_async_copy(wq_hbm.at[:, pl.ds((u - 4) * 256, 256)], w.at[u], w_sem.at[u, 0])]
+        return [
+            pltpu.make_async_copy(src.at[:, pl.ds(u * DH, DH)], w.at[u, :, pl.ds(n * DH, DH)], w_sem.at[u, n])
+            for n, src in enumerate((wk_hbm, wv_hbm))
+        ]
+
+    def start_w(u):
+        for cp in w_cp(u):
+            cp.start()
 
     lam_cp = pltpu.make_async_copy(lam_hbm, lam_raw, misc_sem.at[0])
     prior_cp = pltpu.make_async_copy(prior_hbm, prior, misc_sem.at[1])
@@ -93,27 +100,25 @@
     def z_comes(d):
         return (y_id < 3) | (z_id > d)
 
-    def kv_post(p):
-        for i in range(2):
-            h = 2 * p + i
-            raw = acc[2 * p, :, i * DH:(i + 1) * DH]
-            k_s[h] = (raw * lax.rsqrt(jnp.sum(raw * raw, axis=-1, keepdims=True) + eps)).astype(BF16)
-            vt_s[h] = acc[2 * p + 1, :, i * DH:(i + 1) * DH].T.astype(BF16)
-            st = [
-                dot(vt_s[h, :, c * CH:(c + 1) * CH], k_s[h, c * CH:(c + 1) * CH, :])
-                for c in range(NC)
-            ]
-            s01 = st[0] + st[1]
-            chunk_st[h, 0] = st[0].astype(BF16)
-            chunk_st[h, 1] = s01.astype(BF16)
-            chunk_st[h, 2] = st[2].astype(BF16)
-            total = s01 + (st[2] + st[3])
-            state[h] = total
-            z_send[h] = total.astype(BF16)
-            for d in range(3):
-                @pl.when(z_sends(d))
-                def _():
-                    z_copy(d, h).start()
+    def kv_post(h):
+        raw = acc[h, :, :DH]
+        k_s[h] = (raw * lax.rsqrt(jnp.sum(raw * raw, axis=-1, keepdims=True) + eps)).astype(BF16)
+        vt_s[h] = acc[h, :, DH:].T.astype(BF16)
+        st = [
+            dot(vt_s[h, :, c * CH:(c + 1) * CH], k_s[h, c * CH:(c + 1) * CH, :])
+            for c in range(NC)
+        ]
+        s01 = st[0] + st[1]
+        chunk_st[h, 0] = st[0].astype(BF16)
+        chunk_st[h, 1] = s01.astype(BF16)
+        chunk_st[h, 2] = st[2].astype(BF16)
+        total = s01 + (st[2] + st[3])
+        state[h] = total
+        z_send[h] = total.astype(BF16)
+        for d in range(3):
+            @pl.when(z_sends(d))
+            def _():
+                z_copy(d, h).start()
 
     def pass_on(h):
         for d in range(3):
@@ -188,30 +193,37 @@
 
     def first_cp(k):
         rows = pl.ds(pl.multiple_of(k * TC, TC), TC)
-        return pltpu.make_async_copy(wk_hbm.at[rows, pl.ds(0, 256)], w.at[0, rows, :], first_sem.at[k])
+        return [
+            pltpu.make_async_copy(
+                src.at[rows, pl.ds(0, DH)], w.at[0, rows, pl.ds(n * DH, DH)], first_sem.at[k, n]
+            )
+            for n, src in enumerate((wk_hbm, wv_hbm))
+        ]
 
     for i in range(D // TC):
         tok_cp(i).start()
-        first_cp(i).start()
-    w_cp(1).start()
+        for cp in first_cp(i):
+            cp.start()
+    start_w(1)
     acc[0] = jnp.zeros((ROWS, 256), F32)
 
     def first_unit(k, _):
         part = pl.ds(pl.multiple_of(k * TC, TC), TC)
         pltpu.make_async_copy(tok_hbm.at[:, part], tok.at[:, part], tok_sem.at[k]).wait()
-        first_cp(k).wait()
+        for cp in first_cp(k):
+            cp.wait()
         acc[0] += dot(tok[:, part], w[0, part, :])
         return 0
 
     lax.fori_loop(0, D // TC, first_unit, 0)
-    w_cp(2).start()
-    w_cp(3).start()
+    start_w(2)
+    start_w(3)
 
     def unit(u, _):
         @pl.when(u == 2)
         def _():
-            w_cp(4).start()
-            w_cp(5).start()
+            start_w(4)
+            start_w(5)
             lam_cp.start()
             prior_cp.start()
             gain_cp.start()
@@ -221,21 +233,35 @@
             for b in range(8):
                 wo_cp[b].start()
 
-        pltpu.make_async_copy(wk_hbm.at[:, pl.ds(0, 256)], w.at[u], w_sem.at[u]).wait()
+        @pl.when(u < 4)
+        def _():
+            for n in range(2):
+                pltpu.make_async_copy(
+                    wk_hbm.at[:, pl.ds(0, DH)], w.at[u, :, pl.ds(n * DH, DH)], w_sem.at[u, n]
+                ).wait()
+
+        @pl.when(u >= 4)
+        def _():
+            pltpu.make_async_copy(wq_hbm.at[:, pl.ds(0, 256)], w.at[u], w_sem.at[u, 0]).wait()
+
         acc[u] = dot(tok[...], w[u])
 
         @pl.when(u == 1)
         def _():
             pl.semaphore_wait(barrier, 9)
-
-        @pl.when((u == 1) | (u == 3))
-        def _():
-            kv_post(u // 2)
+            kv_post(0)
+
+        @pl.when(u < 4)
+        def _():
+            kv_post(u)
 
         @pl.when(u >= 4)
         def _():
             q_post(u - 4)
-            pass_on(u - 4)
+
+        @pl.when((u > 3) | ((u == 3) & (z_id > 0)))
+        def _():
+            pass_on(u - 3 - (z_id == 0).astype(jnp.int32))
         return 0
 
     lax.fori_loop(1, 6, unit, 0)
@@ -249,15 +275,13 @@
         near(2 * i)
         near(2 * i + 1)
 
-        @pl.when((i == 0) & (z_id == 0))
-        def _():
-            pass_on(2)
-            pass_on(3)
+        @pl.when(z_id == 0)
+        def _():
+            pass_on(2 + i)
         return 0
 
     @pl.when(z_id > 0)
     def _():
-        pass_on(2)
         pass_on(3)
 
     lax.fori_loop(0, 2, near_step, 0)
@@ -292,9 +316,10 @@
         here = normed[rows_of(n), :]
         for o in (2, 1, 3, 0):
             sib_send[o, n] = dot(here, wo[((x_id + o) % 4) * 2 + 1 - c_id]).astype(BF16)
-            own_p[o, n] = dot(here, wo[((x_id + o) % 4) * 2 + c_id])
         for o in (2, 1, 3, 0):
             sib_copy(o, n).start()
+        for o in (2, 1, 3, 0):
+            own_p[o, n] = dot(here, wo[((x_id + o) % 4) * 2 + c_id])
 
     def chip_sum(n):
         for o in (2, 1, 3, 0):
@@ -426,8 +451,8 @@
         pltpu.VMEM(half, BF16),
         pltpu.VMEM((NS, SUB, 512), BF16),
         pltpu.SemaphoreType.DMA((4,)),
-        pltpu.SemaphoreType.DMA((4,)),
-        pltpu.SemaphoreType.DMA((6,)),
+        pltpu.SemaphoreType.DMA((4, 2)),
+        pltpu.SemaphoreType.DMA((6, 2)),
         pltpu.SemaphoreType.DMA((8,)),
         pltpu.SemaphoreType.DMA((3,)),
         pltpu.SemaphoreType.DMA((NS,)),

time: 47.2 us -> 47 us (level)
  no operation moved by 1% of the time
where the time goes in v6:
time: 47 us; the launch traced here: 46.8 us
  Pallas kernels  44.9 us (96%)
  local copies, waits for them, and re-layouts  1.87 us (4%)
    pallas_call x1, Pallas kernels, per_device(): pl.pallas_call(kernel, out_shape=jax.ShapeDtypeStruct((ROWS, 512), BF16),...  44.9 us
    unnamed x1, local copies, waits for them, and re-layouts  1.87 us

profile of v6, /device:TPU:24, one launch (start us, length us, event | category | flops | bytes accessed | tf_op | source)
XLA Modules:
  0.0 46.8 jit_solution(15171756636591285543)
XLA Ops:
  0.0 44.9 %shard_map.82 = bf16[512,512]{1,0:T(8,128)(2,1)} custom-call(bf16[512,4096]{1,0:T(8,128)(2,1)} %tok_hbm.1, bf16[4096,512]{1,0:T(8,128)(2,1)} %wq_hbm.1, bf16[4096,512]{1,0:T(8,128)(2,1)} %wk_hbm.1, bf16[4096,512]{1,0:T(8,128)(2,1)} %wv_hbm.1, bf16[512,4096]{1,0:T(8,128)(2,1)} %wo_hbm.1, f32[1,512]{1,0:T(1,128)} %bitcast.1, f32[21,4,512]{2,1,0:T(4,128)} %lam_hbm.1, ...), custom_call_target="tpu_custom_call" | custom-call | flops 9500000256 | bytes 22000000 | tf_op jit(solution)/shard_map/pallas_call | solution.py:467
  45.0 1.9 %copy.10 = bf16[512,512]{1,0:T(8,128)(2,1)} copy(bf16[512,512]{1,0:T(8,128)(2,1)} %shard_map.82) | data formatting | bytes 1048576

commit v7 on v6

--- a/solution.py
+++ b/solution.py
@@ -55,10 +55,6 @@
         pl.semaphore_signal(barrier, inc=1, device_id=(((y_id + d) % 4) * 4 + z_id, h_id), device_id_type=MESH)
 
     TC = 1024
-
-    def tok_cp(i):
-        cols = pl.ds(i * TC, TC)
-        return pltpu.make_async_copy(tok_hbm.at[:, cols], tok.at[:, cols], tok_sem.at[i])
 
     def w_cp(u):
         if u >= 4:
@@ -182,7 +178,7 @@
         return [first] + [jnp.where(at > d, 1.0, 0.0) * high for d in (1, 2)]
 
     def finish(h, part):
-        toks = pl.ds(pl.multiple_of(part * 256, 256), 256)
+        toks = pl.ds(pl.multiple_of(part * CH, CH), CH)
         qf = qt_s[h, :, toks].astype(F32)
         rows = far_rows(z_id, SHIFT + 1, h, toks) + far_rows(y_id, SHIFT + 3, h, toks)
         b_all = jnp.concatenate([(row * qf).astype(BF16) for row in rows], axis=0)
@@ -200,11 +196,14 @@
             for n, src in enumerate((wk_hbm, wv_hbm))
         ]
 
-    for i in range(D // TC):
-        tok_cp(i).start()
-        for cp in first_cp(i):
+    def start_first(k):
+        part = pl.ds(pl.multiple_of(k * TC, TC), TC)
+        pltpu.make_async_copy(tok_hbm.at[:, part], tok.at[:, part], tok_sem.at[k]).start()
+        for cp in first_cp(k):
             cp.start()
-    start_w(1)
+
+    start_first(0)
+    start_first(1)
     acc[0] = jnp.zeros((ROWS, 256), F32)
 
     def first_unit(k, _):
@@ -212,23 +211,41 @@
         pltpu.make_async_copy(tok_hbm.at[:, part], tok.at[:, part], tok_sem.at[k]).wait()
         for cp in first_cp(k):
             cp.wait()
+
+        @pl.when(k < 2)
+        def _():
+            start_first(k + 2)
+
+        @pl.when(k == 2)
+        def _():
+            start_w(1)
+
+        @pl.when(k == 3)
+        def _():
+            start_w(2)
+
         acc[0] += dot(tok[:, part], w[0, part, :])
         return 0
 
     lax.fori_loop(0, D // TC, first_unit, 0)
-    start_w(2)
-    start_w(3)
 
     def unit(u, _):
+        @pl.when(u == 1)
+        def _():
+            start_w(3)
+
         @pl.when(u == 2)
         def _():
             start_w(4)
+
+        @pl.when(u == 3)
+        def _():
             start_w(5)
             lam_cp.start()
             prior_cp.start()
             gain_cp.start()
 
-        @pl.when(u == 3)
+        @pl.when(u == 4)
         def _():
             for b in range(8):
                 wo_cp[b].start()
@@ -321,8 +338,8 @@
         for o in (2, 1, 3, 0):
             own_p[o, n] = dot(here, wo[((x_id + o) % 4) * 2 + c_id])
 
-    def chip_sum(n):
-        for o in (2, 1, 3, 0):
+    def chip_sum(n, blocks):
+        for o in blocks:
             sib_copy(o, n).wait_recv()
             total = (own_p[o, n] + sib_recv[o, n].astype(F32)).astype(BF16)
             csum[o, n, 0] = total[:, :W]
@@ -333,36 +350,29 @@
             elif o != 0:
                 x_copy(1, 0 if o == 1 else 1, n).start()
 
+    def wait_y(h, _):
+        for d in range(3):
+            @pl.when(y_id > d)
+            def _():
+                y_copy(d, h).wait_recv()
+        return 0
+
+    lax.fori_loop(0, HEADS, wait_y, 0)
+
     def stage(n, _):
-        @pl.when(n % 2 == 0)
-        def _():
-            @pl.when(n == 0)
-            def _():
-                def wait_y(h, _):
-                    for d in range(3):
-                        @pl.when(y_id > d)
-                        def _():
-                            y_copy(d, h).wait_recv()
-                    return 0
-
-                lax.fori_loop(0, HEADS, wait_y, 0)
-
-            @pl.when(n < NS)
-            def _():
-                def two(i, _):
-                    finish(2 * i, n // 2)
-                    finish(2 * i + 1, n // 2)
-                    return 0
-
-                lax.fori_loop(0, 2, two, 0)
-
         @pl.when(n < NS)
         def _():
+            for h in range(HEADS):
+                finish(h, n)
             project_out(n)
 
         @pl.when(n > 0)
         def _():
-            chip_sum(n - 1)
+            chip_sum(n - 1, (1, 3, 0))
+
+        @pl.when(n < NS)
+        def _():
+            chip_sum(n, (2,))
         return 0
 
     lax.fori_loop(0, NS + 1, stage, 0)

time: 47 us -> 47.3 us (level)
  no operation moved by 1% of the time
where the time goes in v7:
time: 47.3 us; the launch traced here: 46.9 us
  Pallas kernels  45 us (95%)
  local copies, waits for them, and re-layouts  1.87 us (4%)
    pallas_call x1, Pallas kernels, per_device(): pl.pallas_call(kernel, out_shape=jax.ShapeDtypeStruct((ROWS, 512), BF16),...  45 us
    unnamed x1, local copies, waits for them, and re-layouts  1.87 us

profile of v7, /device:TPU:24, one launch (start us, length us, event | category | flops | bytes accessed | tf_op | source)
XLA Modules:
  0.0 46.9 jit_solution(7205444232728629354)
XLA Ops:
  0.0 45.0 %shard_map.82 = bf16[512,512]{1,0:T(8,128)(2,1)} custom-call(bf16[512,4096]{1,0:T(8,128)(2,1)} %tok_hbm.1, bf16[4096,512]{1,0:T(8,128)(2,1)} %wq_hbm.1, bf16[4096,512]{1,0:T(8,128)(2,1)} %wk_hbm.1, bf16[4096,512]{1,0:T(8,128)(2,1)} %wv_hbm.1, bf16[512,4096]{1,0:T(8,128)(2,1)} %wo_hbm.1, f32[1,512]{1,0:T(1,128)} %bitcast.1, f32[21,4,512]{2,1,0:T(4,128)} %lam_hbm.1, ...), custom_call_target="tpu_custom_call" | custom-call | flops 9500000256 | bytes 22000000 | tf_op jit(solution)/shard_map/pallas_call | solution.py:477
  45.0 1.9 %copy.10 = bf16[512,512]{1,0:T(8,128)(2,1)} copy(bf16[512,512]{1,0:T(8,128)(2,1)} %shard_map.82) | data formatting | bytes 1048576

commit v8 on v7

--- a/solution.py
+++ b/solution.py
@@ -177,8 +177,8 @@
         first = odd.astype(F32) * low + jnp.where((odd == 0) & (at > 0), 1.0, 0.0) * high
         return [first] + [jnp.where(at > d, 1.0, 0.0) * high for d in (1, 2)]
 
-    def finish(h, part):
-        toks = pl.ds(pl.multiple_of(part * CH, CH), CH)
+    def finish(h, part, size):
+        toks = pl.ds(pl.multiple_of(part * size, size), size)
         qf = qt_s[h, :, toks].astype(F32)
         rows = far_rows(z_id, SHIFT + 1, h, toks) + far_rows(y_id, SHIFT + 3, h, toks)
         b_all = jnp.concatenate([(row * qf).astype(BF16) for row in rows], axis=0)
@@ -202,8 +202,9 @@
         for cp in first_cp(k):
             cp.start()
 
-    start_first(0)
-    start_first(1)
+    for k in range(D // TC):
+        start_first(k)
+    start_w(1)
     acc[0] = jnp.zeros((ROWS, 256), F32)
 
     def first_unit(k, _):
@@ -212,17 +213,10 @@
         for cp in first_cp(k):
             cp.wait()
 
-        @pl.when(k < 2)
-        def _():
-            start_first(k + 2)
-
-        @pl.when(k == 2)
-        def _():
-            start_w(1)
-
         @pl.when(k == 3)
         def _():
             start_w(2)
+            start_w(3)
 
         acc[0] += dot(tok[:, part], w[0, part, :])
         return 0
@@ -230,22 +224,15 @@
     lax.fori_loop(0, D // TC, first_unit, 0)
 
     def unit(u, _):
-        @pl.when(u == 1)
-        def _():
-            start_w(3)
-
         @pl.when(u == 2)
         def _():
             start_w(4)
-
-        @pl.when(u == 3)
-        def _():
             start_w(5)
             lam_cp.start()
             prior_cp.start()
             gain_cp.start()
 
-        @pl.when(u == 4)
+        @pl.when(u == 3)
         def _():
             for b in range(8):
                 wo_cp[b].start()
@@ -350,20 +337,24 @@
             elif o != 0:
                 x_copy(1, 0 if o == 1 else 1, n).start()
 
-    def wait_y(h, _):
+    def wait_y(h):
         for d in range(3):
             @pl.when(y_id > d)
             def _():
                 y_copy(d, h).wait_recv()
-        return 0
-
-    lax.fori_loop(0, HEADS, wait_y, 0)
+
+    def early_head(h, _):
+        wait_y(h)
+        finish(h, 0, ROWS)
+        return 0
+
+    lax.fori_loop(0, HEADS - 1, early_head, 0)
+    wait_y(HEADS - 1)
 
     def stage(n, _):
         @pl.when(n < NS)
         def _():
-            for h in range(HEADS):
-                finish(h, n)
+            finish(HEADS - 1, n, SUB)
             project_out(n)
 
         @pl.when(n > 0)

time: 47.3 us -> 46.2 us (0.977)
  Pallas kernels: 45 us -> 43.9 us
    pallas_call x1, Pallas kernels: 45 us -> 43.9 us  [per_device(): pl.pallas_call(kernel, out_shape=jax.ShapeDtypeStruct((ROWS, 512), BF16),...]
where the time goes in v8:
time: 46.2 us; the launch traced here: 45.8 us
  Pallas kernels  43.9 us (95%)
  local copies, waits for them, and re-layouts  1.87 us (4%)
    pallas_call x1, Pallas kernels, per_device(): pl.pallas_call(kernel, out_shape=jax.ShapeDtypeStruct((ROWS, 512), BF16),...  43.9 us
    unnamed x1, local copies, waits for them, and re-layouts  1.87 us

profile of v8, /device:TPU:24, one launch (start us, length us, event | category | flops | bytes accessed | tf_op | source)
XLA Modules:
  0.0 45.8 jit_solution(1115820673152869480)
XLA Ops:
  0.0 43.9 %shard_map.82 = bf16[512,512]{1,0:T(8,128)(2,1)} custom-call(bf16[512,4096]{1,0:T(8,128)(2,1)} %tok_hbm.1, bf16[4096,512]{1,0:T(8,128)(2,1)} %wq_hbm.1, bf16[4096,512]{1,0:T(8,128)(2,1)} %wk_hbm.1, bf16[4096,512]{1,0:T(8,128)(2,1)} %wv_hbm.1, bf16[512,4096]{1,0:T(8,128)(2,1)} %wo_hbm.1, f32[1,512]{1,0:T(1,128)} %bitcast.1, f32[21,4,512]{2,1,0:T(4,128)} %lam_hbm.1, ...), custom_call_target="tpu_custom_call" | custom-call | flops 9500000256 | bytes 22000000 | tf_op jit(solution)/shard_map/pallas_call | solution.py:468
  43.9 1.9 %copy.10 = bf16[512,512]{1,0:T(8,128)(2,1)} copy(bf16[512,512]{1,0:T(8,128)(2,1)} %shard_map.82) | data formatting | bytes 1048576

commit v9 on v8

--- a/solution.py
+++ b/solution.py
@@ -111,7 +111,7 @@
         total = s01 + (st[2] + st[3])
         state[h] = total
         z_send[h] = total.astype(BF16)
-        for d in range(3):
+        for d in (1, 0, 2):
             @pl.when(z_sends(d))
             def _():
                 z_copy(d, h).start()
@@ -126,7 +126,7 @@
         def _():
             got = [zy_recv[h, :, d * DH:(d + 1) * DH].astype(F32) for d in range(3)]
             y_send[h] = (state[h] + (got[0] + got[1] + got[2])).astype(BF16)
-            for d in range(3):
+            for d in (1, 0, 2):
                 @pl.when(y_id + 1 + d < 4)
                 def _():
                     y_copy(d, h).start()

time: 46.2 us -> 46.1 us (level)
  no operation moved by 1% of the time
where the time goes in v9:
time: 46.1 us; the launch traced here: 45.7 us
  Pallas kernels  43.8 us (95%)
  local copies, waits for them, and re-layouts  1.87 us (4%)
    pallas_call x1, Pallas kernels, per_device(): pl.pallas_call(kernel, out_shape=jax.ShapeDtypeStruct((ROWS, 512), BF16),...  43.8 us
    unnamed x1, local copies, waits for them, and re-layouts  1.87 us

profile of v9, /device:TPU:24, one launch (start us, length us, event | category | flops | bytes accessed | tf_op | source)
XLA Modules:
  0.0 45.7 jit_solution(6066214365153179771)
XLA Ops:
  0.0 43.8 %shard_map.82 = bf16[512,512]{1,0:T(8,128)(2,1)} custom-call(bf16[512,4096]{1,0:T(8,128)(2,1)} %tok_hbm.1, bf16[4096,512]{1,0:T(8,128)(2,1)} %wq_hbm.1, bf16[4096,512]{1,0:T(8,128)(2,1)} %wk_hbm.1, bf16[4096,512]{1,0:T(8,128)(2,1)} %wv_hbm.1, bf16[512,4096]{1,0:T(8,128)(2,1)} %wo_hbm.1, f32[1,512]{1,0:T(1,128)} %bitcast.1, f32[21,4,512]{2,1,0:T(4,128)} %lam_hbm.1, ...), custom_call_target="tpu_custom_call" | custom-call | flops 9500000256 | bytes 22000000 | tf_op jit(solution)/shard_map/pallas_call | solution.py:468
  43.8 1.9 %copy.10 = bf16[512,512]{1,0:T(8,128)(2,1)} copy(bf16[512,512]{1,0:T(8,128)(2,1)} %shard_map.82) | data formatting | bytes 1048576
